TPU v7x, 32 devices: a whole 2x2x4 slice. The times are simulated.
32 devices in a mesh: group: 2 (over x), shard: 16 (over z, y, core).
Axes of the slice: x: 2, y: 2, z: 4, core: 2. Of those that a mesh axis runs over, the one named last changes fastest.
Arguments:
- inner_embed: float32 [2, 15360, 768], P('group', 'shard'), may hold values from -6 to 6
- outer_embed: float32 [15360, 768], P('shard'), may hold values from -6 to 6
- moment_embed: float32 [15360, 768], P('shard'), may hold values from -6 to 6
- basis: float32 [15360, 64], P('shard'), may hold values from -6 to 6
- inner_attn: float32 [2, 768, 3072], P('group', 'shard'), may hold values from -6 to 6
- outer_attn: float32 [768, 3072], P(None, 'shard'), may hold values from -6 to 6
- moment_attn: float32 [768, 3072], P(None, 'shard'), may hold values from -6 to 6
- inner_norms: float32 [2, 4, 768], P('group', None, 'shard'), may hold values from -6 to 6
- outer_norms: float32 [4, 768], P(None, 'shard'), may hold values from -6 to 6
- moment_norms: float32 [4, 768], P(None, 'shard'), may hold values from -6 to 6
Outputs:
- new_embed: float32 [15360, 768], P('shard')
- new_moment_embed: float32 [15360, 768], P('shard')
- new_attn: float32 [768, 3072], P(None, 'shard')
- new_moment_attn: float32 [768, 3072], P(None, 'shard')
- new_norms: float32 [4, 768], P(None, 'shard')
- new_moment_norms: float32 [4, 768], P(None, 'shard')
- replica_attn: bfloat16 [768, 3072], P('shard')
All inputs are finite; a program needn't handle non-finite values.
Results may differ from a plain program's by a relative error of at most 0.0004.
Values may be sent and summed in bfloat16 or wider, within the bound.
No kernel may reach another device: no remote copies, remote signals or barrier semaphores. Data moves between devices by JAX's collectives and lax.ppermute only.
A program may use at most 64 MiB of HBM per device.

v0:
```python
import math

import jax
import jax.numpy as jnp
from jax import lax
from jax.sharding import PartitionSpec as P

VOCAB = 15360
RANK = 64


def nesterov(outer, moment, delta):
    moment_new = 0.5 * moment + delta
    return (outer - (delta + 0.5 * moment_new), moment_new)


def on_device(
    inner_embed,
    outer_embed,
    moment_embed,
    basis,
    inner_attn,
    outer_attn,
    moment_attn,
    inner_norms,
    outer_norms,
    moment_norms,
):
    groups = lax.axis_size("group")
    embed_diff = outer_embed - inner_embed[0]
    partial_coeff = lax.dot_general(
        basis,
        embed_diff,
        (((0,), (0,)), ((), ())),
        precision=lax.Precision.HIGHEST,
        preferred_element_type=jnp.float32,
    )
    norm_diff = outer_norms - inner_norms[0]
    moved = lax.all_to_all(inner_attn[0], "shard", split_axis=1, concat_axis=0, tiled=True)
    attn_term = outer_attn - moved
    coeff_sum = lax.psum(partial_coeff, ("group", "shard"))
    attn_sum, norm_sum = lax.psum((attn_term, norm_diff), "group")
    attn_delta = attn_sum / groups
    norm_delta = norm_sum / groups
    coefficient = coeff_sum / groups
    embed_delta = jnp.dot(
        basis, coefficient, precision=lax.Precision.HIGHEST, preferred_element_type=jnp.float32
    ) * (1.0 / math.sqrt(RANK * VOCAB))
    new_embed, new_moment_embed = nesterov(outer_embed, moment_embed, embed_delta)
    new_attn, new_moment_attn = nesterov(outer_attn, moment_attn, attn_delta)
    new_norms, new_moment_norms = nesterov(outer_norms, moment_norms, norm_delta)
    replica_attn = lax.all_to_all(
        new_attn.astype(jnp.bfloat16), "shard", split_axis=0, concat_axis=1, tiled=True
    )
    return (
        new_embed,
        new_moment_embed,
        new_attn,
        new_moment_attn,
        new_norms,
        new_moment_norms,
        replica_attn,
    )


def solution(mesh):
    placed = (
        P("group", "shard", None),
        P("shard", None),
        P("shard", None),
        P("shard", None),
        P("group", "shard", None),
        P(None, "shard"),
        P(None, "shard"),
        P("group", None, "shard"),
        P(None, "shard"),
        P(None, "shard"),
    )
    return jax.shard_map(
        on_device,
        mesh=mesh,
        in_specs=placed,
        out_specs=(
            P("shard", None),
            P("shard", None),
            P(None, "shard"),
            P(None, "shard"),
            P(None, "shard"),
            P(None, "shard"),
            P("shard", None),
        ),
        check_vma=False,
    )
```

profile of v0, /device:TPU:0, one launch (start us, length us, event | category | flops | bytes accessed | tf_op | source)
XLA Modules:
  0.0 225.9 jit_solution(12121702814765061931)
XLA Ops:
  7.2 0.0 copy-start
  7.2 1.5 all_to_all.28
  8.6 1.3 copy.25
  10.0 0.0 copy-start.1
  10.0 7.7 %all-to-all-start = ((f32[48,16,192]{2,0,1:T(8,128)}), f32[48,16,192]{2,0,1:T(8,128)}, u32[]{:S(2)}, u32[]{:S(2)}) async-start(f32[48,16,192]{2,0,1:T(8,128)} %copy.25), calls=%async_computation | async-start | bytes 1572864 | tf_op jit(solution)/shard_map/all_to_all | solution.py:39
  17.7 0.0 all-reduce.5.cloned.1.call-start
  17.7 2.2 copy.28
  20.0 16.5 %all-to-all-done = f32[48,16,192]{2,0,1:T(8,128)} async-done(((f32[48,16,192]{2,0,1:T(8,128)}), f32[48,16,192]{2,0,1:T(8,128)}, u32[]{:S(2)}, u32[]{:S(2)}) %all-to-all-start) | async-done | bytes 589856 | tf_op jit(solution)/shard_map/all_to_all | solution.py:39
  36.5 2.4 %bitcast_subtract_fusion.4 = f32[768,192]{1,0:T(8,128)} fusion(f32[768,192]{1,0:T(8,128)} %copy.28, f32[48,16,192]{2,0,1:T(8,128)} %all-to-all-done), kind=kLoop, calls=%fused_computation.6 | loop fusion | flops 147456 | bytes 1769472 | tf_op jit(solution)/shard_map/sub | solution.py:40
  38.8 0.0 all-reduce.5.cloned.1.call-update
  38.9 0.0 copy-start.2
  38.9 0.0 copy-start.3
  38.9 0.0 all-reduce.3.cloned.1.call-start
  38.9 0.0 copy-done
  38.9 0.0 copy-done.1
  39.0 4.5 %fusion.2 = f32[64,768]{1,0:T(8,128)} fusion(f32[960,64]{0,1:T(8,128)S(1)} %copy-done, f32[960,768]{1,0:T(8,128)S(1)} %copy-done.1, f32[1,960,768]{2,1,0:T(8,128)} %param.10), kind=kOutput, calls=%fused_computation.5 | convolution fusion | flops 566968320 | bytes 6340608 | tf_op jit(solution)/shard_map/dot_general | solution.py:31
  43.5 0.0 all-reduce.3.cloned.1.call-update
  43.5 0.0 copy-start.4
  43.5 2.2 copy.27
  45.7 0.0 copy-done.2
  45.7 0.0 copy-done.3
  45.7 5.0 %psum.23 = f32[4,48]{1,0:T(4,128)S(1)} all-reduce(f32[4,48]{1,0:T(4,128)S(1)} %bitcast_subtract_fusion.5), channel_id=1, replica_groups=mesh['group'=2,'shard'=16] {'group'}, use_global_device_ids=true, to_apply=%region_2.0 | all-reduce | flops 192 | bytes 1536 | tf_op jit(solution)/shard_map/psum | solution.py:42
  50.7 23.5 %all-reduce.5.cloned.1.call-done = f32[768,192]{1,0:T(8,128)} async-done(((f32[768,192]{1,0:T(8,128)}), f32[768,192]{1,0:T(8,128)}) %all-reduce.5.cloned.1.call-update) | async-done | bytes 589840 | tf_op jit(solution)/shard_map/psum | solution.py:42
  74.2 3.1 %fusion.7 = (bf16[768,192]{1,0:T(8,128)(2,1)}, f32[768,192]{1,0:T(8,128)}, f32[768,192]{1,0:T(8,128)}) fusion(f32[768,192]{1,0:T(8,128)} %copy.28, f32[768,192]{1,0:T(8,128)} %copy.27, f32[768,192]{1,0:T(8,128)} %all-reduce.5.cloned.1.call-done), kind=kLoop, calls=%fused_computation.16 | loop fusion | flops 1032192 | bytes 3244032 | tf_op jit(solution)/shard_map/convert_element_type | solution.py:53
  77.3 5.7 %all-to-all-start.1 = ((bf16[16,48,192]{2,1,0:T(8,128)(2,1)}), bf16[16,48,192]{2,1,0:T(8,128)(2,1)}, u32[]{:S(2)}, u32[]{:S(2)}) async-start(bf16[16,48,192]{2,1,0:T(8,128)(2,1)} %bitcast.23), calls=%async_computation.1 | async-start | bytes 786432 | tf_op jit(solution)/shard_map/all_to_all | solution.py:52
  83.0 0.0 copy-done.4
  83.0 0.6 add_subtract_fusion.1
  83.6 121.5 %all-reduce.3.cloned.1.call-done = f32[64,768]{1,0:T(8,128)} async-done(((f32[64,768]{1,0:T(8,128)}), f32[64,768]{1,0:T(8,128)}) %all-reduce.3.cloned.1.call-update) | async-done | bytes 196624 | tf_op jit(solution)/shard_map/psum | solution.py:41
  205.0 7.4 %fusion = (f32[960,768]{1,0:T(8,128)}, f32[960,768]{1,0:T(8,128)}) fusion(f32[960,768]{1,0:T(8,128)S(1)} %copy-done.1, f32[960,768]{1,0:T(8,128)} %param.12, f32[960,64]{0,1:T(8,128)S(1)} %copy-done, f32[64,768]{1,0:T(8,128)} %all-reduce.3.cloned.1.call-done), kind=kOutput, calls=%fused_computation.2 | convolution fusion | flops 570703872 | bytes 12238848 | tf_op jit(solution)/shard_map/dot_general | solution.py:46
  212.5 2.2 copy.30
  214.7 2.2 copy.31
  216.9 0.0 all-to-all-done.1
  216.9 1.1 copy.29
  218.0 1.1 all_to_all.35
  (1 shorter events, 0.0 us)
Async XLA Ops:
  7.2 31.8 %copy-start = (f32[960,64]{0,1:T(8,128)S(1)}, f32[960,64]{0,1:T(8,128)}, u32[]{:S(2)}) copy-start(f32[960,64]{0,1:T(8,128)} %param.13) | copy-start | bytes 737284
  10.0 29.0 %copy-start.1 = (f32[960,768]{1,0:T(8,128)S(1)}, f32[960,768]{1,0:T(8,128)}, u32[]{:S(2)}) copy-start(f32[960,768]{1,0:T(8,128)} %param.11) | copy-start | bytes 8847364
  10.0 26.5 %all-to-all-start = ((f32[48,16,192]{2,0,1:T(8,128)}), f32[48,16,192]{2,0,1:T(8,128)}, u32[]{:S(2)}, u32[]{:S(2)}) async-start(f32[48,16,192]{2,0,1:T(8,128)} %copy.25), calls=%async_computation | async-start | bytes 1572864 | tf_op jit(solution)/shard_map/all_to_all | solution.py:39
  17.7 56.5 %all-reduce.5.cloned.1.call-start = ((), (), s32[]{:S(2)}) async-start(), calls=%async_computation.3 | async-start | bytes 1572864 | tf_op jit(solution)/shard_map/psum | solution.py:42
  38.9 6.9 %copy-start.2 = (f32[4,48]{1,0:T(4,128)S(1)}, f32[4,48]{1,0:T(4,128)}, u32[]{:S(2)}) copy-start(f32[4,48]{1,0:T(4,128)} %param.18) | copy-start | bytes 2308
  38.9 6.9 %copy-start.3 = (f32[1,4,48]{2,1,0:T(4,128)S(1)}, f32[1,4,48]{2,1,0:T(4,128)}, u32[]{:S(2)}) copy-start(f32[1,4,48]{2,1,0:T(4,128)} %param.17) | copy-start | bytes 2308
  38.9 166.2 %all-reduce.3.cloned.1.call-start = ((), (), s32[]{:S(2)}) async-start(), calls=%async_computation.2 | async-start | bytes 393216 | tf_op jit(solution)/shard_map/psum | solution.py:41
  43.5 39.5 %copy-start.4 = (f32[4,48]{1,0:T(4,128)S(1)}, f32[4,48]{1,0:T(4,128)}, u32[]{:S(2)}) copy-start(f32[4,48]{1,0:T(4,128)} %param.19) | copy-start | bytes 2308
  77.3 139.6 %all-to-all-start.1 = ((bf16[16,48,192]{2,1,0:T(8,128)(2,1)}), bf16[16,48,192]{2,1,0:T(8,128)(2,1)}, u32[]{:S(2)}, u32[]{:S(2)}) async-start(bf16[16,48,192]{2,1,0:T(8,128)(2,1)} %bitcast.23), calls=%async_computation.1 | async-start | bytes 786432 | tf_op jit(solution)/shard_map/all_to_all | solution.py:52
Sparse Core Ops, SparseCore 0:
  39.0 35.1 all-reduce.4
  81.3 123.7 all-reduce.2
where the time goes:
time: 227 us; the launch traced here: 226 us
  waiting for transfers between devices  161 us (71%)
  between operations  14.1 us (6%)
  local copies, waits for them, and re-layouts  13.9 us (6%)
  starting transfers between devices  13.4 us (6%)
  matrix products  12 us (5%)
  other arithmetic  6.04 us (3%)
  blocking collectives  5 us (2%)
    psum x1, waiting for transfers between devices, on_device(): coeff_sum = lax.psum(partial_coeff, ('group', 'shard'))  121 us
    psum x1, waiting for transfers between devices, on_device(): attn_sum, norm_sum = lax.psum((attn_term, norm_diff), 'group')  23.5 us
    all_to_all x1, waiting for transfers between devices, on_device(): lax.all_to_all(inner_attn[0], 'shard', split_axis=1, concat_axis=0, tiled...  16.5 us
    unnamed x14, local copies, waits for them, and re-layouts  8.86 us
    all_to_all x1, starting transfers between devices, on_device(): lax.all_to_all(inner_attn[0], 'shard', split_axis=1, concat_axis=0, tiled...  7.69 us
    dot_general x1, matrix products, on_device(): jnp.dot(basis, coefficient, precision=lax.Precision.HIGHEST, preferred_el...  7.45 us
    all_to_all x1, starting transfers between devices, on_device(): lax.all_to_all(new_attn.astype(jnp.bfloat16), 'shard', split_axis=0, conc...  5.66 us
    psum x1, blocking collectives, on_device(): attn_sum, norm_sum = lax.psum((attn_term, norm_diff), 'group')  5 us
  transfers between devices with their start and end apart: 4, of which 3 were waited for; matrix products, arithmetic and copies ran while one was open for 11% of the time, Pallas kernels for 0%

commit v1 on v0

v1 whole, which is shorter than its diff:
```python
import functools
import math

import jax
import jax.numpy as jnp
from jax import lax
from jax.experimental import pallas as pl
from jax.experimental.pallas import tpu as pltpu
from jax.sharding import PartitionSpec as P

VOCAB = 15360
RANK = 64
LANES = 128
HALF = 64
ROWS = 40

f32 = jnp.float32
bf16 = jnp.bfloat16
VMEM = pltpu.VMEM
LIMIT = 40 * 1024 * 1024


def nesterov(outer, moment, delta):
    moment_new = 0.5 * moment + delta
    return (outer - (delta + 0.5 * moment_new), moment_new)


def remote(count):
    return [pl.BlockSpec(memory_space=pltpu.HBM)] * count


def cost(flops, moved):
    return pl.CostEstimate(flops=flops, bytes_accessed=moved, transcendentals=0)


def left_half(shape):
    return lax.broadcasted_iota(jnp.int32, shape, 1) < HALF


def roll_half(x):
    return pltpu.roll(x, HALF, 1)


def split3(x):
    hi = x.astype(bf16)
    lo = (x - hi.astype(f32)).astype(bf16)
    return hi, lo


def dot3(a, b, dims):
    ah, al = split3(a)
    bh, bl = split3(b)
    mul = functools.partial(lax.dot_general, dimension_numbers=(dims, ((), ())), preferred_element_type=f32)
    return mul(ah, bh) + (mul(ah, bl) + mul(al, bh))


def chunks(rows):
    return [(at, min(256, rows - at)) for at in range(0, rows, 256)]


def coeff_kernel(basis_in, outer_in, inner_in, mine_ref, other_ref, basis_ref, outer_ref, inner_ref, sems):
    parts = chunks(outer_ref.shape[0])

    def copy(src, dst, at, size, sem):
        return pltpu.make_async_copy(src.at[pl.ds(at, size)], dst.at[pl.ds(at, size)], sems.at[sem])

    copies = [copy(basis_in, basis_ref, 0, basis_ref.shape[0], 0)]
    for k, (at, size) in enumerate(parts):
        copies.append(copy(outer_in, outer_ref, at, size, 1 + 2 * k))
        copies.append(copy(inner_in, inner_ref, at, size, 2 + 2 * k))
    for c in copies:
        c.start()
    copies[0].wait()
    first = lax.rem(lax.axis_index("shard"), 2) == 0
    rows = mine_ref.shape[0]
    total = None
    for k, (at, size) in enumerate(parts):
        copies[1 + 2 * k].wait()
        copies[2 + 2 * k].wait()
        part = slice(at, at + size)
        term = dot3(basis_ref[:, part], outer_ref[part, :] - inner_ref[part, :], ((1,), (0,)))
        total = term if total is None else total + term
    low, high = total[:rows], total[rows:]
    other_ref[...] = jnp.where(first, high, low)
    mine_ref[...] = jnp.where(first, low, high)


def norm_tile(scr, norm_ref):
    scr[...] = jnp.zeros_like(scr)
    scr[: norm_ref.shape[0], : norm_ref.shape[1]] = norm_ref[...]
    return roll_half(scr[...])


def make_piece(main, half, tile):
    mask = left_half((8, LANES))
    third = jnp.where(mask, half[0:8], roll_half(half[8:16]))
    return jnp.concatenate([main, third, jnp.where(mask, half[16:24], tile)], axis=0)


def put_piece(out_ref, at, main, half, tile):
    out_ref[at] = make_piece(main, half, tile)


def get_half(piece):
    return jnp.concatenate([piece[24:32], roll_half(piece[24:32]), piece[32:40]], axis=0)


def pack_kernel(shards, load, store, x_ref, norm_ref, out_ref, scr):
    load(1)
    tile = norm_tile(scr, norm_ref)
    mask = left_half((24, LANES))
    for group in range(2):
        load(0, group)
        rows = slice(24 * group, 24 * group + 24)
        for pair in range(shards // 2):
            at = group * shards + 2 * pair
            t = [x_ref[rows, 384 * pair + LANES * k : 384 * pair + LANES * k + LANES] for k in range(3)]
            t1, t2 = roll_half(t[1]), roll_half(t[2])
            put_piece(out_ref, at, t[0], t[1], tile)
            put_piece(out_ref, at + 1, jnp.where(mask, t1, t2), t2, tile)
        store(0, slice(group * shards, group * shards + shards))


def states_kernel(shards, load, store, outer_ref, moment_ref, outer_norm_ref, moment_norm_ref, outer_out, moment_out, scr, tile_scr):
    group = lax.axis_index("group")
    for n, (src, norm, out) in enumerate(((outer_ref, outer_norm_ref, outer_out), (moment_ref, moment_norm_ref, moment_out))):
        load(2 + n)
        tile = norm_tile(tile_scr, norm)
        load(n)
        for k in range(src.shape[1] // LANES):
            cols = slice(LANES * k, LANES * k + LANES)
            scr[n, cols, 0:LANES] = src[0:LANES, cols].T
            scr[n, cols, LANES : LANES + HALF] = src[LANES : LANES + HALF, cols].T
        for s in range(shards):
            rows = pl.ds(pl.multiple_of(48 * s + 24 * group, 8), 24)
            out[s] = make_piece(scr[n, rows, :LANES], scr[n, rows, LANES:], tile)
        store(n)


def middle_kernel(shards, load, store, outer_ref, moment_ref, got_ref, send_ref, delta_ref):
    for n in range(3):
        load(n)
    for s in range(shards):
        outer = outer_ref[s]
        delta = ((outer - got_ref[s]) + (outer - got_ref[shards + s])) * 0.5
        delta_ref[s] = delta
        new = nesterov(outer, moment_ref[s], delta)[0].astype(bf16)
        send_ref[s] = new
        send_ref[shards + s] = new
    store(0)
    store(1)


def last_kernel(shards, scale, embed, load, store, *refs):
    n_in = len(LAST_IN)
    r = dict(zip(LAST_IN + LAST_OUT, refs))
    scr = refs[len(r)]
    at_in = {name: n for n, name in enumerate(LAST_IN)}
    at_out = {name: n for n, name in enumerate(LAST_OUT)}
    group, me = lax.axis_index("group"), lax.axis_index("shard")
    for name in ("coeff_mine", "coeff_other", "basis"):
        load(at_in[name])
    first = lax.rem(me, 2) == 0
    mine, other = r["coeff_mine"][...], r["coeff_other"][...]
    coeff = jnp.concatenate([jnp.where(first, mine, other), jnp.where(first, other, mine)], axis=0) * scale
    for k, (at, size) in enumerate(embed):
        part = slice(at, at + size)
        delta = dot3(r["basis"][:, part], coeff, ((0,), (0,)))
        load(at_in["outer_embed"], k)
        load(at_in["moment_embed"], k)
        r["new_embed"][part, :], r["new_moment_embed"][part, :] = nesterov(
            r["outer_embed"][part, :], r["moment_embed"][part, :], delta
        )
        store(at_out["new_embed"], part)
        store(at_out["new_moment_embed"], part)
    load(at_in["got"])
    mask = left_half((24, LANES))
    for pair in range(shards // 2):
        tiles = [[], [], []]
        for g in range(2):
            even, odd = (r["got"][g * shards + 2 * pair + n].astype(f32) for n in range(2))
            turned = roll_half(odd[0:24])
            tiles[0].append(even[0:24])
            tiles[1].append(jnp.where(mask, get_half(even), turned))
            tiles[2].append(jnp.where(mask, turned, roll_half(get_half(odd))))
        for k in range(3):
            at = 384 * pair + LANES * k
            r["replica"][:, at : at + LANES] = jnp.concatenate(tiles[k], axis=0).astype(bf16)
    store(at_out["replica"])
    for name, owner in (("delta_mine", group), ("delta_other", 1 - group)):
        load(at_in[name])
        for s in range(shards):
            piece = r[name][s]
            rows = pl.ds(pl.multiple_of(48 * s + 24 * owner, 8), 24)
            scr[rows, 0:LANES] = piece[0:24]
            scr[rows, LANES : 2 * LANES] = get_half(piece)
    for name in ("outer_attn", "moment_attn", "outer_norms", "moment_norms"):
        load(at_in[name])
    for k in range(r["outer_attn"].shape[1] // LANES):
        cols = slice(LANES * k, LANES * k + LANES)
        for rows, part in ((slice(0, LANES), scr[cols, 0:LANES].T), (slice(LANES, LANES + HALF), scr[cols, LANES : 2 * LANES].T[:HALF])):
            r["new_attn"][rows, cols], r["new_moment_attn"][rows, cols] = nesterov(
                r["outer_attn"][rows, cols], r["moment_attn"][rows, cols], part
            )
    store(at_out["new_attn"])
    store(at_out["new_moment_attn"])
    tile = roll_half(r["delta_mine"][me, 32:40, :])
    norms, width = r["outer_norms"].shape
    r["new_norms"][...], r["new_moment_norms"][...] = nesterov(
        r["outer_norms"][...], r["moment_norms"][...], tile[:norms, :width]
    )
    store(at_out["new_norms"])
    store(at_out["new_moment_norms"])


LAST_IN = (
    "coeff_mine", "coeff_other", "basis", "outer_embed", "moment_embed", "got", "delta_mine", "delta_other",
    "outer_attn", "moment_attn", "outer_norms", "moment_norms",
)
LAST_OUT = ("new_embed", "new_moment_embed", "new_attn", "new_moment_attn", "new_norms", "new_moment_norms", "replica")


def staged(kernel, parts, count, *refs):
    ins, outs = refs[: len(parts)], refs[len(parts) : count]
    scratch = list(refs[count:])
    held_in = [scratch.pop(0) if p else ref for p, ref in zip(parts, ins, strict=True)]
    held_out = [scratch.pop(0) for _ in outs]
    in_sem, out_sem = scratch.pop(0), scratch.pop(0)

    def copy(n, k):
        at, size = parts[n][k]
        part = slice(at, at + size)
        return pltpu.make_async_copy(ins[n].at[part], held_in[n].at[part], in_sem.at[sum(len(p) for p in parts[:n]) + k])

    for k in range(max(len(p) for p in parts)):
        for n in range(len(parts)):
            if k < len(parts[n]):
                copy(n, k).start()

    def load(n, k=0):
        if parts[n]:
            copy(n, k).wait()

    def store(n, part=slice(None)):
        pltpu.make_async_copy(held_out[n].at[part], outs[n].at[part], out_sem.at[n]).start()

    kernel(load, store, *held_in, *held_out, *scratch)
    for n in range(len(outs)):
        pltpu.make_async_copy(held_out[n], outs[n], out_sem.at[n]).wait()


def call(kernel, args, outs, scratch=(), flops=0, parts=None, here=()):
    moved = sum(x.size * x.dtype.itemsize for x in args) + sum(math.prod(s) * jnp.dtype(d).itemsize for s, d in outs)
    parts = parts or {}
    parts = [[] if n in here else parts.get(n, [(0, x.shape[0])]) for n, x in enumerate(args)]
    return pl.pallas_call(
        functools.partial(staged, kernel, parts, len(args) + len(outs)),
        out_shape=[pltpu.HBM(s, d) for s, d in outs],
        in_specs=[pl.BlockSpec(memory_space=pltpu.HBM if p else VMEM) for p in parts],
        out_specs=remote(len(outs)),
        scratch_shapes=[pltpu.VMEM(x.shape, x.dtype) for x, p in zip(args, parts, strict=True) if p]
        + [pltpu.VMEM(s, d) for s, d in outs]
        + [pltpu.SemaphoreType.DMA((sum(len(p) for p in parts),)), pltpu.SemaphoreType.DMA((len(outs),))]
        + list(scratch),
        compiler_params=pltpu.CompilerParams(vmem_limit_bytes=LIMIT),
        cost_estimate=cost(flops, moved),
    )(*[pltpu.with_memory_space_constraint(x, pltpu.HBM) if p else x for x, p in zip(args, parts, strict=True)])


def after(x, *others):
    return lax.optimization_barrier((x, *others))[0]


def everyone(x):
    return lax.all_to_all(x, ("group", "shard"), split_axis=0, concat_axis=0, tiled=True)


def swap_groups(x):
    return lax.ppermute(x, "group", [(0, 1), (1, 0)])


def swap_shards(x, bit):
    return lax.ppermute(x, "shard", [(i, i ^ bit) for i in range(lax.axis_size("shard"))])


def fast(
    inner_embed, outer_embed, moment_embed, basis, inner_attn, outer_attn, moment_attn,
    inner_norms, outer_norms, moment_norms,
):
    shards = lax.axis_size("shard")
    rows, width = outer_embed.shape
    rank = basis.shape[1]
    basis = basis.T
    outer_attn, moment_attn = outer_attn.T, moment_attn.T
    piece = (shards, ROWS, LANES)

    (sent,) = call(
        functools.partial(pack_kernel, shards), (inner_attn[0], inner_norms[0]), [((2 * shards, ROWS, LANES), f32)],
        [pltpu.VMEM((8, LANES), f32)], parts={0: [(0, 24), (24, 24)]},
    )
    got = everyone(sent)

    mine, other = pl.pallas_call(
        coeff_kernel,
        out_shape=[jax.ShapeDtypeStruct((rank // 2, width), f32)] * 2,
        in_specs=remote(3),
        out_specs=[pl.BlockSpec(memory_space=VMEM)] * 2,
        scratch_shapes=[pltpu.VMEM(basis.shape, f32)]
        + [pltpu.VMEM(outer_embed.shape, f32)] * 2
        + [pltpu.SemaphoreType.DMA((1 + 2 * len(chunks(rows)),))],
        compiler_params=pltpu.CompilerParams(vmem_limit_bytes=LIMIT),
        cost_estimate=cost(6 * rank * rows * width, 8 * rows * width),
    )(*[pltpu.with_memory_space_constraint(x, pltpu.HBM) for x in (basis, outer_embed, inner_embed[0])])
    mine = mine + swap_shards(other, 1)
    steps = [mine]
    mine = mine + swap_groups(mine)
    steps.append(mine)
    bit = 2
    while bit < shards:
        mine = mine + swap_shards(mine, bit)
        steps.append(mine)
        bit *= 2
    other = swap_shards(mine, 1)

    outer_piece, moment_piece = call(
        functools.partial(states_kernel, shards), (outer_attn, moment_attn, outer_norms, moment_norms), [(piece, f32)] * 2,
        [pltpu.VMEM((2, outer_attn.shape[1], 2 * LANES), f32), pltpu.VMEM((8, LANES), f32)],
    )
    send, delta = call(
        functools.partial(middle_kernel, shards), (after(outer_piece, steps[2]), moment_piece, got),
        [((2 * shards, ROWS, LANES), bf16), (piece, f32)], here=(2,),
    )
    replica = everyone(send)
    delta_other = swap_groups(delta)
    embed = chunks(rows)
    new_embed, new_moment_embed, new_attn, new_moment_attn, new_norms, new_moment_norms, replica_attn = call(
        functools.partial(last_kernel, shards, 0.5 / math.sqrt(RANK * VOCAB), embed),
        (mine, other, basis, outer_embed, moment_embed, replica, delta, delta_other, outer_attn, moment_attn, outer_norms, moment_norms),
        [((rows, width), f32)] * 2 + [(outer_attn.shape, f32)] * 2 + [(outer_norms.shape, f32)] * 2 + [(inner_attn.shape[1:], bf16)],
        [pltpu.VMEM((outer_attn.shape[1], 2 * LANES), f32)], flops=6 * rank * rows * width, parts={3: embed, 4: embed}, here=(0, 1, 5, 7),
    )
    return (new_embed, new_moment_embed, new_attn.T, new_moment_attn.T, new_norms, new_moment_norms, replica_attn)


def plain(
    inner_embed, outer_embed, moment_embed, basis, inner_attn, outer_attn, moment_attn,
    inner_norms, outer_norms, moment_norms,
):
    groups = lax.axis_size("group")
    coeff = lax.dot_general(
        basis, outer_embed - inner_embed[0], (((0,), (0,)), ((), ())),
        precision=lax.Precision.HIGHEST, preferred_element_type=f32,
    )
    moved = lax.all_to_all(inner_attn[0], "shard", split_axis=1, concat_axis=0, tiled=True)
    coeff = lax.psum(coeff, ("group", "shard")) / groups
    attn_sum, norm_sum = lax.psum((outer_attn - moved, outer_norms - inner_norms[0]), "group")
    embed_delta = jnp.dot(basis, coeff, precision=lax.Precision.HIGHEST, preferred_element_type=f32) * (
        1.0 / math.sqrt(RANK * VOCAB)
    )
    new_embed, new_moment_embed = nesterov(outer_embed, moment_embed, embed_delta)
    new_attn, new_moment_attn = nesterov(outer_attn, moment_attn, attn_sum / groups)
    new_norms, new_moment_norms = nesterov(outer_norms, moment_norms, norm_sum / groups)
    replica_attn = lax.all_to_all(new_attn.astype(bf16), "shard", split_axis=0, concat_axis=1, tiled=True)
    return (new_embed, new_moment_embed, new_attn, new_moment_attn, new_norms, new_moment_norms, replica_attn)


def on_device(*args):
    outer_embed, basis, inner_attn, outer_attn, norms = args[1], args[3], args[4], args[5], args[8]
    shards = lax.axis_size("shard")
    fits = (
        lax.axis_size("group") == 2
        and shards >= 2
        and shards & (shards - 1) == 0
        and inner_attn.shape == (1, 48, 192 * shards)
        and outer_attn.shape == (48 * shards, 192)
        and outer_attn.shape[0] % LANES == 0
        and norms.shape[0] <= 8
        and norms.shape[1] <= HALF
        and outer_embed.shape[1] % 256 == 0
        and outer_embed.shape[0] % 8 == 0
        and basis.shape[1] % 16 == 0
    )
    return (fast if fits else plain)(*args)


def solution(mesh):
    placed = (
        P("group", "shard", None),
        P("shard", None),
        P("shard", None),
        P("shard", None),
        P("group", "shard", None),
        P(None, "shard"),
        P(None, "shard"),
        P("group", None, "shard"),
        P(None, "shard"),
        P(None, "shard"),
    )
    return jax.shard_map(
        on_device,
        mesh=mesh,
        in_specs=placed,
        out_specs=(
            P("shard", None),
            P("shard", None),
            P(None, "shard"),
            P(None, "shard"),
            P(None, "shard"),
            P(None, "shard"),
            P("shard", None),
        ),
        check_vma=False,
    )
```

time: 227 us -> 59.8 us (0.26)
  waiting for transfers between devices: 161 us -> 21.5 us
  Pallas kernels: 0 us -> 16.7 us
  local copies, waits for them, and re-layouts: 13.9 us -> 0 us
  between operations: 14.1 us -> 0.71 us
  matrix products: 12 us -> 0 us
  starting transfers between devices: 13.4 us -> 20.5 us
  other arithmetic: 6.04 us -> 0.06 us
  blocking collectives: 5 us -> 0 us
    psum x2 -> x0, waiting for transfers between devices: 145 us -> none  [the longest x1 121 us: on_device(): coeff_sum = lax.psum(partial_coeff, ('group', 'shard'))]
    ppermute x0 -> x7, waiting for transfers between devices: none -> 19 us  [the longest x5 14.2 us: swap_shards(): lax.ppermute(x, 'shard', [(i, i ^ bit) for i in range(lax.axis_size('shar...]
    pallas_call x0 -> x5, Pallas kernels: none -> 16.7 us  [the longest x4 13.5 us: call(): pl.pallas_call(functools.partial(staged, kernel, parts, len(args) + len(o...]
    all_to_all x2, waiting for transfers between devices: 16.5 us -> 2.54 us  [everyone(): lax.all_to_all(x, ('group', 'shard'), split_axis=0, concat_axis=0, tiled=...]
    dot_general x2 -> x0, matrix products: 12 us -> none  [the longest x1 7.45 us: on_device(): jnp.dot(basis, coefficient, precision=lax.Precision.HIGHEST, preferred_el...]
    ppermute x0 -> x7, starting transfers between devices: none -> 10 us  [the longest x5 6.35 us: swap_shards(): lax.ppermute(x, 'shard', [(i, i ^ bit) for i in range(lax.axis_size('shar...]
    unnamed x14 -> x0, local copies, waits for them, and re-layouts: 8.86 us -> none
    all_to_all x4 -> x0, local copies, waits for them, and re-layouts: 5 us -> none  [the longest x2 2.8 us: on_device(): lax.all_to_all(inner_attn[0], 'shard', split_axis=1, concat_axis=0, tiled...]
  transfers between devices with their start and end apart: 4 -> 9, of which waited for: 3 -> 7; matrix products, arithmetic and copies ran while one was open for 11% -> 0% of each run, Pallas kernels for 0% -> 10%
where the time goes in v1:
time: 59.8 us; the launch traced here: 59.4 us
  waiting for transfers between devices  21.5 us (36%)
  starting transfers between devices  20.5 us (34%)
  Pallas kernels  16.7 us (28%)
  between operations  0.71 us (1%)
    ppermute x5, waiting for transfers between devices, swap_shards(): lax.ppermute(x, 'shard', [(i, i ^ bit) for i in range(lax.axis_size('shar...  14.2 us
    pallas_call x4, Pallas kernels, call(): pl.pallas_call(functools.partial(staged, kernel, parts, len(args) + len(o...  13.5 us
    all_to_all x2, starting transfers between devices, everyone(): lax.all_to_all(x, ('group', 'shard'), split_axis=0, concat_axis=0, tiled=...  10.5 us
    ppermute x5, starting transfers between devices, swap_shards(): lax.ppermute(x, 'shard', [(i, i ^ bit) for i in range(lax.axis_size('shar...  6.35 us
    ppermute x2, waiting for transfers between devices, swap_groups(): return lax.ppermute(x, 'group', [(0, 1), (1, 0)])  4.71 us
    ppermute x2, starting transfers between devices, swap_groups(): return lax.ppermute(x, 'group', [(0, 1), (1, 0)])  3.67 us
    pallas_call x1, Pallas kernels, fast(): pl.pallas_call(coeff_kernel, out_shape=[jax.ShapeDtypeStruct((rank // 2,...  3.14 us
    all_to_all x2, waiting for transfers between devices, everyone(): lax.all_to_all(x, ('group', 'shard'), split_axis=0, concat_axis=0, tiled=...  2.54 us
  transfers between devices with their start and end apart: 9, of which 7 were waited for; matrix products, arithmetic and copies ran while one was open for 0% of the time, Pallas kernels for 10%

profile of v1, /device:TPU:0, one launch (start us, length us, event | category | flops | bytes accessed | tf_op | source)
XLA Modules:
  0.0 59.4 jit_solution(1561933363668688561)
XLA Ops:
  0.6 2.0 %shard_map.155 = f32[32,40,128]{2,1,0:T(8,128)} custom-call(f32[48,3072]{1,0:T(8,128)} %bitcast.15, f32[4,48]{1,0:T(4,128)} %bitcast.16), custom_call_target="tpu_custom_call" | custom-call | bytes 1245952 | tf_op jit(solution)/shard_map/pallas_call | solution.py:256
  2.7 7.3 %all-to-all-start = ((f32[32,40,128]{2,1,0:T(8,128)}), f32[32,40,128]{2,1,0:T(8,128)S(1)}, u32[]{:S(2)}, u32[]{:S(2)}) async-start(f32[32,40,128]{2,1,0:T(8,128)} %shard_map.155), calls=%async_computation | async-start | bytes 1310720 | tf_op jit(solution)/shard_map/all_to_all | solution.py:275
  10.0 3.1 %shard_map.153 = (f32[32,768]{1,0:T(8,128)S(1)}, f32[32,768]{1,0:T(8,128)S(1)}) custom-call(f32[64,960]{1,0:T(8,128)} %bitcast.13, f32[960,768]{1,0:T(8,128)} %refs_3_.3, f32[960,768]{1,0:T(8,128)} %bitcast.8), custom_call_target="tpu_custom_call" | custom-call | flops 283115520 | bytes 5898240 | tf_op jit(solution)/shard_map/pallas_call | solution.py:303
  13.1 0.3 collective-permute-start
  13.4 1.1 %collective-permute-done = f32[32,768]{1,0:T(8,128)S(1)} collective-permute-done((f32[32,768]{1,0:T(8,128)S(1)}, f32[32,768]{1,0:T(8,128)S(1)}, u32[]{:S(2)}, u32[]{:S(2)}) %collective-permute-start) | collective-permute-done | bytes 98336 | tf_op jit(solution)/shard_map/ppermute | solution.py:283
  14.5 1.8 %collective-permute-start.1 = (f32[32,768]{1,0:T(8,128)S(1)}, f32[32,768]{1,0:T(8,128)S(1)}, u32[]{:S(2)}, u32[]{:S(2)}) collective-permute-start(f32[32,768]{1,0:T(8,128)S(1)} %add.15), channel_id=1, source_target_pairs={{0,16},{16,0},{1,17},{17,1},{2,18},{18,2},{3,19},{19,3},{4,20},{20... | collective-permute-start | bytes 294920 | tf_op jit(solution)/shard_map/ppermute | solution.py:279
  16.3 4.7 %collective-permute-done.1 = f32[32,768]{1,0:T(8,128)S(1)} collective-permute-done((f32[32,768]{1,0:T(8,128)S(1)}, f32[32,768]{1,0:T(8,128)S(1)}, u32[]{:S(2)}, u32[]{:S(2)}) %collective-permute-start.1) | collective-permute-done | bytes 98336 | tf_op jit(solution)/shard_map/ppermute | solution.py:279
  21.1 1.4 %collective-permute-start.2 = (f32[32,768]{1,0:T(8,128)S(1)}, f32[32,768]{1,0:T(8,128)S(1)}, u32[]{:S(2)}, u32[]{:S(2)}) collective-permute-start(f32[32,768]{1,0:T(8,128)S(1)} %add.16), channel_id=1, source_target_pairs={{0,2},{1,3},{2,0},{3,1},{4,6},{5,7},{6,4},{7,5},{8,10},{9,11},{10,... | collective-permute-start | bytes 294920 | tf_op jit(solution)/shard_map/ppermute | solution.py:283
  22.4 2.8 %shard_map.154 = (f32[16,40,128]{2,1,0:T(8,128)}, f32[16,40,128]{2,1,0:T(8,128)}) custom-call(f32[192,768]{1,0:T(8,128)} %bitcast.9, f32[192,768]{1,0:T(8,128)} %bitcast.11, f32[4,48]{1,0:T(4,128)} %refs_10_.1, f32[4,48]{1,0:T(4,128)} %refs_11_.1), custom_call_target="tpu_custom_call" | custom-call | bytes 1836544 | tf_op jit(solution)/shard_map/pallas_call | solution.py:256
  25.2 0.9 %collective-permute-done.2 = f32[32,768]{1,0:T(8,128)S(1)} collective-permute-done((f32[32,768]{1,0:T(8,128)S(1)}, f32[32,768]{1,0:T(8,128)S(1)}, u32[]{:S(2)}, u32[]{:S(2)}) %collective-permute-start.2) | collective-permute-done | bytes 98336 | tf_op jit(solution)/shard_map/ppermute | solution.py:283
  26.2 2.5 %all-to-all-done.refs_2_ = f32[32,40,128]{2,1,0:T(8,128)S(1)} async-done(((f32[32,40,128]{2,1,0:T(8,128)}), f32[32,40,128]{2,1,0:T(8,128)S(1)}, u32[]{:S(2)}, u32[]{:S(2)}) %all-to-all-start) | async-done | bytes 655392 | tf_op jit(solution)/shard_map/all_to_all | solution.py:275
  28.7 2.0 %shard_map.156 = (bf16[32,40,128]{2,1,0:T(8,128)(2,1)}, f32[16,40,128]{2,1,0:T(8,128)}) custom-call(f32[16,40,128]{2,1,0:T(8,128)} %get-tuple-element.24.refs_0_, f32[16,40,128]{2,1,0:T(8,128)} %get-tuple-element.25.refs_1_, f32[32,40,128]{2,1,0:T(8,128)S(1)} %all-to-all-done.refs_2_), custom_call_target="tpu_custom_call" | custom-call | bytes 1966080 | tf_op jit(solution)/shard_map/pallas_call | solution.py:256
  30.7 3.2 %all-to-all-start.1 = ((bf16[32,40,128]{2,1,0:T(8,128)(2,1)}), bf16[32,40,128]{2,1,0:T(8,128)(2,1)S(1)}, u32[]{:S(2)}, u32[]{:S(2)}) async-start(bf16[32,40,128]{2,1,0:T(8,128)(2,1)} %get-tuple-element.26), calls=%async_computation.1 | async-start | bytes 655360 | tf_op jit(solution)/shard_map/all_to_all | solution.py:275
  33.9 1.8 %collective-permute-start.6 = (f32[16,40,128]{2,1,0:T(8,128)}, f32[16,40,128]{2,1,0:T(8,128)S(1)}, u32[]{:S(2)}, u32[]{:S(2)}) collective-permute-start(f32[16,40,128]{2,1,0:T(8,128)} %get-tuple-element.27.refs_6_), channel_id=1, source_target_pairs={{0,16},{16,0},{1,17},{17,1},{2,18},{18,2},{3,19},{19,3},{4,20},{20... | collective-permute-start | bytes 983048 | tf_op jit(solution)/shard_map/ppermute | solution.py:279
  35.8 1.5 %collective-permute-start.3 = (f32[32,768]{1,0:T(8,128)S(1)}, f32[32,768]{1,0:T(8,128)S(1)}, u32[]{:S(2)}, u32[]{:S(2)}) collective-permute-start(f32[32,768]{1,0:T(8,128)S(1)} %add.17), channel_id=1, source_target_pairs={{0,4},{1,5},{2,6},{3,7},{4,0},{5,1},{6,2},{7,3},{8,12},{9,13},{10,... | collective-permute-start | bytes 294920 | tf_op jit(solution)/shard_map/ppermute | solution.py:283
  37.2 6.3 %collective-permute-done.3 = f32[32,768]{1,0:T(8,128)S(1)} collective-permute-done((f32[32,768]{1,0:T(8,128)S(1)}, f32[32,768]{1,0:T(8,128)S(1)}, u32[]{:S(2)}, u32[]{:S(2)}) %collective-permute-start.3) | collective-permute-done | bytes 98336 | tf_op jit(solution)/shard_map/ppermute | solution.py:283
  43.5 3.1 %collective-permute-start.4 = (f32[32,768]{1,0:T(8,128)S(1)}, f32[32,768]{1,0:T(8,128)S(1)}, u32[]{:S(2)}, u32[]{:S(2)}) collective-permute-start(f32[32,768]{1,0:T(8,128)S(1)} %add.18), channel_id=1, source_target_pairs={{0,8},{1,9},{2,10},{3,11},{4,12},{5,13},{6,14},{7,15},{8,0},{9,1},... | collective-permute-start | bytes 294920 | tf_op jit(solution)/shard_map/ppermute | solution.py:283
  46.7 4.7 %collective-permute-done.4 = f32[32,768]{1,0:T(8,128)S(1)} collective-permute-done((f32[32,768]{1,0:T(8,128)S(1)}, f32[32,768]{1,0:T(8,128)S(1)}, u32[]{:S(2)}, u32[]{:S(2)}) %collective-permute-start.4) | collective-permute-done | bytes 98336 | tf_op jit(solution)/shard_map/ppermute | solution.py:283
  51.4 0.1 collective-permute-start.5
  51.5 1.3 %collective-permute-done.5.refs_1_ = f32[32,768]{1,0:T(8,128)S(1)} collective-permute-done((f32[32,768]{1,0:T(8,128)S(1)}, f32[32,768]{1,0:T(8,128)S(1)}, u32[]{:S(2)}, u32[]{:S(2)}) %collective-permute-start.5) | collective-permute-done | bytes 98336 | tf_op jit(solution)/shard_map/ppermute | solution.py:283
  52.7 0.0 collective-permute-done.6.refs_7_
  52.7 0.0 all-to-all-done.1.refs_5_
  52.7 6.7 %shard_map.157 = (f32[960,768]{1,0:T(8,128)}, f32[960,768]{1,0:T(8,128)}, f32[192,768]{1,0:T(8,128)}, f32[192,768]{1,0:T(8,128)}, f32[4,48]{1,0:T(4,128)}, /*index=5*/f32[4,48]{1,0:T(4,128)}, bf16[48,3072]{1,0:T(8,128)(2,1)}) custom-call(f32[32,768]{1,0:T(8,128)S(1)} %add.19.refs_0_, f32[32,768]{1,0:T(8,128)S(1)} %collective-permute-done.5.refs_1_, ...), custom_call_target="tpu_custom_call" | custom-call | flops 283115520 | bytes 15879168 | tf_op jit(solution)/shard_map/pallas_call | solution.py:256
  (5 shorter events, 0.1 us)
Async XLA Ops:
  2.7 26.0 %all-to-all-start = ((f32[32,40,128]{2,1,0:T(8,128)}), f32[32,40,128]{2,1,0:T(8,128)S(1)}, u32[]{:S(2)}, u32[]{:S(2)}) async-start(f32[32,40,128]{2,1,0:T(8,128)} %shard_map.155), calls=%async_computation | async-start | bytes 1310720 | tf_op jit(solution)/shard_map/all_to_all | solution.py:275
  13.1 1.4 %collective-permute-start = (f32[32,768]{1,0:T(8,128)S(1)}, f32[32,768]{1,0:T(8,128)S(1)}, u32[]{:S(2)}, u32[]{:S(2)}) collective-permute-start(f32[32,768]{1,0:T(8,128)S(1)} %get-tuple-element.22), channel_id=1, source_target_pairs={{0,1},{1,0},{2,3},{3,2},{4,5},{5,4},{6,7},{7,6},{8,9},{9,8},{10,11... | collective-permute-start | bytes 294920 | tf_op jit(solution)/shard_map/ppermute | solution.py:283
  14.5 6.5 %collective-permute-start.1 = (f32[32,768]{1,0:T(8,128)S(1)}, f32[32,768]{1,0:T(8,128)S(1)}, u32[]{:S(2)}, u32[]{:S(2)}) collective-permute-start(f32[32,768]{1,0:T(8,128)S(1)} %add.15), channel_id=1, source_target_pairs={{0,16},{16,0},{1,17},{17,1},{2,18},{18,2},{3,19},{19,3},{4,20},{20... | collective-permute-start | bytes 294920 | tf_op jit(solution)/shard_map/ppermute | solution.py:279
  21.1 5.1 %collective-permute-start.2 = (f32[32,768]{1,0:T(8,128)S(1)}, f32[32,768]{1,0:T(8,128)S(1)}, u32[]{:S(2)}, u32[]{:S(2)}) collective-permute-start(f32[32,768]{1,0:T(8,128)S(1)} %add.16), channel_id=1, source_target_pairs={{0,2},{1,3},{2,0},{3,1},{4,6},{5,7},{6,4},{7,5},{8,10},{9,11},{10,... | collective-permute-start | bytes 294920 | tf_op jit(solution)/shard_map/ppermute | solution.py:283
  30.7 22.0 %all-to-all-start.1 = ((bf16[32,40,128]{2,1,0:T(8,128)(2,1)}), bf16[32,40,128]{2,1,0:T(8,128)(2,1)S(1)}, u32[]{:S(2)}, u32[]{:S(2)}) async-start(bf16[32,40,128]{2,1,0:T(8,128)(2,1)} %get-tuple-element.26), calls=%async_computation.1 | async-start | bytes 655360 | tf_op jit(solution)/shard_map/all_to_all | solution.py:275
  33.9 18.8 %collective-permute-start.6 = (f32[16,40,128]{2,1,0:T(8,128)}, f32[16,40,128]{2,1,0:T(8,128)S(1)}, u32[]{:S(2)}, u32[]{:S(2)}) collective-permute-start(f32[16,40,128]{2,1,0:T(8,128)} %get-tuple-element.27.refs_6_), channel_id=1, source_target_pairs={{0,16},{16,0},{1,17},{17,1},{2,18},{18,2},{3,19},{19,3},{4,20},{20... | collective-permute-start | bytes 983048 | tf_op jit(solution)/shard_map/ppermute | solution.py:279
  35.8 7.8 %collective-permute-start.3 = (f32[32,768]{1,0:T(8,128)S(1)}, f32[32,768]{1,0:T(8,128)S(1)}, u32[]{:S(2)}, u32[]{:S(2)}) collective-permute-start(f32[32,768]{1,0:T(8,128)S(1)} %add.17), channel_id=1, source_target_pairs={{0,4},{1,5},{2,6},{3,7},{4,0},{5,1},{6,2},{7,3},{8,12},{9,13},{10,... | collective-permute-start | bytes 294920 | tf_op jit(solution)/shard_map/ppermute | solution.py:283
  43.5 7.8 %collective-permute-start.4 = (f32[32,768]{1,0:T(8,128)S(1)}, f32[32,768]{1,0:T(8,128)S(1)}, u32[]{:S(2)}, u32[]{:S(2)}) collective-permute-start(f32[32,768]{1,0:T(8,128)S(1)} %add.18), channel_id=1, source_target_pairs={{0,8},{1,9},{2,10},{3,11},{4,12},{5,13},{6,14},{7,15},{8,0},{9,1},... | collective-permute-start | bytes 294920 | tf_op jit(solution)/shard_map/ppermute | solution.py:283
  51.4 1.4 %collective-permute-start.5 = (f32[32,768]{1,0:T(8,128)S(1)}, f32[32,768]{1,0:T(8,128)S(1)}, u32[]{:S(2)}, u32[]{:S(2)}) collective-permute-start(f32[32,768]{1,0:T(8,128)S(1)} %add.19.refs_0_), channel_id=1, source_target_pairs={{0,1},{1,0},{2,3},{3,2},{4,5},{5,4},{6,7},{7,6},{8,9},{9,8},{10,11... | collective-permute-start | bytes 294920 | tf_op jit(solution)/shard_map/ppermute | solution.py:283

commit v2 on v1

--- a/solution.py
+++ b/solution.py
@@ -47,11 +47,12 @@
     return hi, lo
 
 
-def dot3(a, b, dims):
+def dot3(a, b):
+    rows = a.shape[0]
     ah, al = split3(a)
     bh, bl = split3(b)
-    mul = functools.partial(lax.dot_general, dimension_numbers=(dims, ((), ())), preferred_element_type=f32)
-    return mul(ah, bh) + (mul(ah, bl) + mul(al, bh))
+    both = jnp.dot(jnp.concatenate([ah, al], axis=0), bh, preferred_element_type=f32)
+    return both[:rows] + (both[rows:] + jnp.dot(ah, bl, preferred_element_type=f32))
 
 
 def chunks(rows):
@@ -78,7 +79,7 @@
         copies[1 + 2 * k].wait()
         copies[2 + 2 * k].wait()
         part = slice(at, at + size)
-        term = dot3(basis_ref[:, part], outer_ref[part, :] - inner_ref[part, :], ((1,), (0,)))
+        term = dot3(basis_ref[:, part], outer_ref[part, :] - inner_ref[part, :])
         total = term if total is None else total + term
     low, high = total[:rows], total[rows:]
     other_ref[...] = jnp.where(first, high, low)
@@ -151,73 +152,72 @@
     store(1)
 
 
-def last_kernel(shards, scale, embed, load, store, *refs):
-    n_in = len(LAST_IN)
-    r = dict(zip(LAST_IN + LAST_OUT, refs))
-    scr = refs[len(r)]
-    at_in = {name: n for n, name in enumerate(LAST_IN)}
-    at_out = {name: n for n, name in enumerate(LAST_OUT)}
-    group, me = lax.axis_index("group"), lax.axis_index("shard")
-    for name in ("coeff_mine", "coeff_other", "basis"):
-        load(at_in[name])
-    first = lax.rem(me, 2) == 0
-    mine, other = r["coeff_mine"][...], r["coeff_other"][...]
-    coeff = jnp.concatenate([jnp.where(first, mine, other), jnp.where(first, other, mine)], axis=0) * scale
-    for k, (at, size) in enumerate(embed):
+def join_kernel(scale, mine_ref, other_ref, out_ref):
+    first = lax.rem(lax.axis_index("shard"), 2) == 0
+    mine, other = mine_ref[...] * scale, other_ref[...] * scale
+    high, low = split3(jnp.concatenate([jnp.where(first, mine, other), jnp.where(first, other, mine)], axis=0))
+    out_ref[...] = jnp.concatenate([high, low, high], axis=0)
+
+
+def embed_kernel(parts, load, store, coeff_ref, basis_ref, outer_ref, moment_ref, new_ref, new_moment_ref):
+    coeff = coeff_ref[...]
+    load(1)
+    for k, (at, size) in enumerate(parts):
         part = slice(at, at + size)
-        delta = dot3(r["basis"][:, part], coeff, ((0,), (0,)))
-        load(at_in["outer_embed"], k)
-        load(at_in["moment_embed"], k)
-        r["new_embed"][part, :], r["new_moment_embed"][part, :] = nesterov(
-            r["outer_embed"][part, :], r["moment_embed"][part, :], delta
-        )
-        store(at_out["new_embed"], part)
-        store(at_out["new_moment_embed"], part)
-    load(at_in["got"])
+        high, low = split3(basis_ref[:, part])
+        three = jnp.concatenate([high, high, low], axis=0)
+        delta = lax.dot_general(three, coeff, (((0,), (0,)), ((), ())), preferred_element_type=f32)
+        load(2, k)
+        load(3, k)
+        new_ref[part, :], new_moment_ref[part, :] = nesterov(outer_ref[part, :], moment_ref[part, :], delta)
+        store(0, part)
+        store(1, part)
+
+
+def replica_kernel(shards, load, store, got_ref, out_ref):
     mask = left_half((24, LANES))
     for pair in range(shards // 2):
         tiles = [[], [], []]
         for g in range(2):
-            even, odd = (r["got"][g * shards + 2 * pair + n].astype(f32) for n in range(2))
+            even, odd = (got_ref[g * shards + 2 * pair + n].astype(f32) for n in range(2))
             turned = roll_half(odd[0:24])
             tiles[0].append(even[0:24])
             tiles[1].append(jnp.where(mask, get_half(even), turned))
             tiles[2].append(jnp.where(mask, turned, roll_half(get_half(odd))))
         for k in range(3):
             at = 384 * pair + LANES * k
-            r["replica"][:, at : at + LANES] = jnp.concatenate(tiles[k], axis=0).astype(bf16)
-    store(at_out["replica"])
-    for name, owner in (("delta_mine", group), ("delta_other", 1 - group)):
-        load(at_in[name])
+            out_ref[:, at : at + LANES] = jnp.concatenate(tiles[k], axis=0).astype(bf16)
+        if pair % 2:
+            store(0, (slice(None), slice(384 * pair - 384, 384 * pair + 384)))
+
+
+def attn_kernel(
+    shards, load, store, mine_ref, other_ref, outer_ref, moment_ref, outer_norm_ref, moment_norm_ref,
+    new_ref, new_moment_ref, new_norm_ref, new_moment_norm_ref, scr,
+):
+    group, me = lax.axis_index("group"), lax.axis_index("shard")
+    for n, (src, owner) in enumerate(((mine_ref, group), (other_ref, 1 - group))):
+        load(n)
         for s in range(shards):
-            piece = r[name][s]
+            piece = src[s]
             rows = pl.ds(pl.multiple_of(48 * s + 24 * owner, 8), 24)
             scr[rows, 0:LANES] = piece[0:24]
             scr[rows, LANES : 2 * LANES] = get_half(piece)
-    for name in ("outer_attn", "moment_attn", "outer_norms", "moment_norms"):
-        load(at_in[name])
-    for k in range(r["outer_attn"].shape[1] // LANES):
+    for n in range(2, 6):
+        load(n)
+    for k in range(outer_ref.shape[1] // LANES):
         cols = slice(LANES * k, LANES * k + LANES)
         for rows, part in ((slice(0, LANES), scr[cols, 0:LANES].T), (slice(LANES, LANES + HALF), scr[cols, LANES : 2 * LANES].T[:HALF])):
-            r["new_attn"][rows, cols], r["new_moment_attn"][rows, cols] = nesterov(
-                r["outer_attn"][rows, cols], r["moment_attn"][rows, cols], part
-            )
-    store(at_out["new_attn"])
-    store(at_out["new_moment_attn"])
-    tile = roll_half(r["delta_mine"][me, 32:40, :])
-    norms, width = r["outer_norms"].shape
-    r["new_norms"][...], r["new_moment_norms"][...] = nesterov(
-        r["outer_norms"][...], r["moment_norms"][...], tile[:norms, :width]
-    )
-    store(at_out["new_norms"])
-    store(at_out["new_moment_norms"])
-
-
-LAST_IN = (
-    "coeff_mine", "coeff_other", "basis", "outer_embed", "moment_embed", "got", "delta_mine", "delta_other",
-    "outer_attn", "moment_attn", "outer_norms", "moment_norms",
-)
-LAST_OUT = ("new_embed", "new_moment_embed", "new_attn", "new_moment_attn", "new_norms", "new_moment_norms", "replica")
+            new_ref[rows, cols], new_moment_ref[rows, cols] = nesterov(outer_ref[rows, cols], moment_ref[rows, cols], part)
+    store(0)
+    store(1)
+    tile = roll_half(mine_ref[me, 32:40, :])
+    norms, width = outer_norm_ref.shape
+    new_norm_ref[...], new_moment_norm_ref[...] = nesterov(
+        outer_norm_ref[...], moment_norm_ref[...], tile[:norms, :width]
+    )
+    store(2)
+    store(3)
 
 
 def staged(kernel, parts, count, *refs):
@@ -249,7 +249,7 @@
         pltpu.make_async_copy(held_out[n], outs[n], out_sem.at[n]).wait()
 
 
-def call(kernel, args, outs, scratch=(), flops=0, parts=None, here=()):
+def call(kernel, args, outs, scratch=(), flops=0, parts=None, here=(), weight=1):
     moved = sum(x.size * x.dtype.itemsize for x in args) + sum(math.prod(s) * jnp.dtype(d).itemsize for s, d in outs)
     parts = parts or {}
     parts = [[] if n in here else parts.get(n, [(0, x.shape[0])]) for n, x in enumerate(args)]
@@ -260,10 +260,10 @@
         out_specs=remote(len(outs)),
         scratch_shapes=[pltpu.VMEM(x.shape, x.dtype) for x, p in zip(args, parts, strict=True) if p]
         + [pltpu.VMEM(s, d) for s, d in outs]
-        + [pltpu.SemaphoreType.DMA((sum(len(p) for p in parts),)), pltpu.SemaphoreType.DMA((len(outs),))]
+        + [pltpu.SemaphoreType.DMA((max(1, sum(len(p) for p in parts)),)), pltpu.SemaphoreType.DMA((len(outs),))]
         + list(scratch),
         compiler_params=pltpu.CompilerParams(vmem_limit_bytes=LIMIT),
-        cost_estimate=cost(flops, moved),
+        cost_estimate=cost(weight * flops, weight * moved),
     )(*[pltpu.with_memory_space_constraint(x, pltpu.HBM) if p else x for x, p in zip(args, parts, strict=True)])
 
 
@@ -312,32 +312,49 @@
         cost_estimate=cost(6 * rank * rows * width, 8 * rows * width),
     )(*[pltpu.with_memory_space_constraint(x, pltpu.HBM) for x in (basis, outer_embed, inner_embed[0])])
     mine = mine + swap_shards(other, 1)
-    steps = [mine]
-    mine = mine + swap_groups(mine)
-    steps.append(mine)
-    bit = 2
-    while bit < shards:
-        mine = mine + swap_shards(mine, bit)
-        steps.append(mine)
-        bit *= 2
-    other = swap_shards(mine, 1)
-
     outer_piece, moment_piece = call(
         functools.partial(states_kernel, shards), (outer_attn, moment_attn, outer_norms, moment_norms), [(piece, f32)] * 2,
         [pltpu.VMEM((2, outer_attn.shape[1], 2 * LANES), f32), pltpu.VMEM((8, LANES), f32)],
     )
-    send, delta = call(
-        functools.partial(middle_kernel, shards), (after(outer_piece, steps[2]), moment_piece, got),
-        [((2 * shards, ROWS, LANES), bf16), (piece, f32)], here=(2,),
-    )
-    replica = everyone(send)
+    steps = []
+    for n, step in enumerate(("x", 4, 8, 2)):
+        moved = swap_groups(mine) if step == "x" else swap_shards(mine, step)
+        if n == 0:
+            moved = after(moved, outer_piece)
+        if n == 2:
+            send, delta = call(
+                functools.partial(middle_kernel, shards), (after(outer_piece, steps[1]), moment_piece, got),
+                [((2 * shards, ROWS, LANES), bf16), (piece, f32)], here=(2,),
+            )
+            moved = after(moved, delta)
+        mine = mine + moved
+        steps.append(mine)
+    other = swap_shards(mine, 1)
+
+    replica = everyone(after(send, steps[2]))
     delta_other = swap_groups(delta)
     embed = chunks(rows)
-    new_embed, new_moment_embed, new_attn, new_moment_attn, new_norms, new_moment_norms, replica_attn = call(
-        functools.partial(last_kernel, shards, 0.5 / math.sqrt(RANK * VOCAB), embed),
-        (mine, other, basis, outer_embed, moment_embed, replica, delta, delta_other, outer_attn, moment_attn, outer_norms, moment_norms),
-        [((rows, width), f32)] * 2 + [(outer_attn.shape, f32)] * 2 + [(outer_norms.shape, f32)] * 2 + [(inner_attn.shape[1:], bf16)],
-        [pltpu.VMEM((outer_attn.shape[1], 2 * LANES), f32)], flops=6 * rank * rows * width, parts={3: embed, 4: embed}, here=(0, 1, 5, 7),
+    coeff = pl.pallas_call(
+        functools.partial(join_kernel, 0.5 / math.sqrt(RANK * VOCAB)),
+        out_shape=jax.ShapeDtypeStruct((3 * rank, width), bf16),
+        in_specs=[pl.BlockSpec(memory_space=VMEM)] * 2,
+        out_specs=pl.BlockSpec(memory_space=VMEM),
+        compiler_params=pltpu.CompilerParams(vmem_limit_bytes=LIMIT),
+        cost_estimate=cost(5 * 10**8, 16 * rank * width),
+    )(mine, other)
+    new_embed, new_moment_embed = call(
+        functools.partial(embed_kernel, embed),
+        (after(coeff, delta_other), basis, outer_embed, moment_embed), [((rows, width), f32)] * 2,
+        flops=6 * rank * rows * width, parts={2: embed, 3: embed}, here=(0,), weight=18,
+    )
+    new_attn, new_moment_attn, new_norms, new_moment_norms = call(
+        functools.partial(attn_kernel, shards),
+        (delta, delta_other, outer_attn, moment_attn, outer_norms, moment_norms),
+        [(outer_attn.shape, f32)] * 2 + [(outer_norms.shape, f32)] * 2,
+        [pltpu.VMEM((outer_attn.shape[1], 2 * LANES), f32)], here=(1,),
+    )
+    (replica_attn,) = call(
+        functools.partial(replica_kernel, shards), (replica,), [(inner_attn.shape[1:], bf16)], here=(0,)
     )
     return (new_embed, new_moment_embed, new_attn.T, new_moment_attn.T, new_norms, new_moment_norms, replica_attn)
 
@@ -374,6 +391,7 @@
         and inner_attn.shape == (1, 48, 192 * shards)
         and outer_attn.shape == (48 * shards, 192)
         and outer_attn.shape[0] % LANES == 0
+        and shards % 4 == 0
         and norms.shape[0] <= 8
         and norms.shape[1] <= HALF
         and outer_embed.shape[1] % 256 == 0

time: 59.8 us -> 51.8 us (0.87)
  waiting for transfers between devices: 21.5 us -> 15 us
  starting transfers between devices: 20.5 us -> 17.4 us
  Pallas kernels: 16.7 us -> 18.3 us
    ppermute x5, waiting for transfers between devices: 14.2 us -> 10.3 us  [swap_shards(): lax.ppermute(x, 'shard', [(i, i ^ bit) for i in range(lax.axis_size('shar...]
    ppermute x2, waiting for transfers between devices: 4.71 us -> 1.95 us  [swap_groups(): return lax.ppermute(x, 'group', [(0, 1), (1, 0)])]
    ppermute x5, starting transfers between devices: 6.35 us -> 3.86 us  [swap_shards(): lax.ppermute(x, 'shard', [(i, i ^ bit) for i in range(lax.axis_size('shar...]
    pallas_call x4 -> x6, Pallas kernels: 13.5 us -> 15.1 us  [call(): pl.pallas_call(functools.partial(staged, kernel, parts, len(args) + len(o...]
    ppermute x2, starting transfers between devices: 3.67 us -> 2.97 us  [swap_groups(): return lax.ppermute(x, 'group', [(0, 1), (1, 0)])]
  transfers between devices with their start and end apart: 9 -> 9, of which waited for: 7 -> 7; matrix products, arithmetic and copies ran while one was open for 0% -> 0% of each run, Pallas kernels for 10% -> 30%
where the time goes in v2:
time: 51.8 us; the launch traced here: 51.5 us
  Pallas kernels  18.3 us (35%)
  starting transfers between devices  17.4 us (34%)
  waiting for transfers between devices  15 us (29%)
  between operations  0.74 us (1%)
    pallas_call x6, Pallas kernels, call(): pl.pallas_call(functools.partial(staged, kernel, parts, len(args) + len(o...  15.1 us
    all_to_all x2, starting transfers between devices, everyone(): lax.all_to_all(x, ('group', 'shard'), split_axis=0, concat_axis=0, tiled=...  10.6 us
    ppermute x5, waiting for transfers between devices, swap_shards(): lax.ppermute(x, 'shard', [(i, i ^ bit) for i in range(lax.axis_size('shar...  10.3 us
    ppermute x5, starting transfers between devices, swap_shards(): lax.ppermute(x, 'shard', [(i, i ^ bit) for i in range(lax.axis_size('shar...  3.86 us
    pallas_call x1, Pallas kernels, fast(): pl.pallas_call(coeff_kernel, out_shape=[jax.ShapeDtypeStruct((rank // 2,...  3.1 us
    ppermute x2, starting transfers between devices, swap_groups(): return lax.ppermute(x, 'group', [(0, 1), (1, 0)])  2.97 us
    all_to_all x2, waiting for transfers between devices, everyone(): lax.all_to_all(x, ('group', 'shard'), split_axis=0, concat_axis=0, tiled=...  2.67 us
    ppermute x2, waiting for transfers between devices, swap_groups(): return lax.ppermute(x, 'group', [(0, 1), (1, 0)])  1.95 us
  transfers between devices with their start and end apart: 9, of which 7 were waited for; matrix products, arithmetic and copies ran while one was open for 0% of the time, Pallas kernels for 30%

profile of v2, /device:TPU:0, one launch (start us, length us, event | category | flops | bytes accessed | tf_op | source)
XLA Modules:
  0.0 51.5 jit_solution(5576547252846285084)
XLA Ops:
  0.6 2.0 %shard_map.155 = f32[32,40,128]{2,1,0:T(8,128)} custom-call(f32[48,3072]{1,0:T(8,128)} %bitcast.13, f32[4,48]{1,0:T(4,128)} %bitcast.16), custom_call_target="tpu_custom_call" | custom-call | bytes 1245952 | tf_op jit(solution)/shard_map/pallas_call | solution.py:256
  2.7 7.3 %all-to-all-start = ((f32[32,40,128]{2,1,0:T(8,128)}), f32[32,40,128]{2,1,0:T(8,128)S(1)}, u32[]{:S(2)}, u32[]{:S(2)}) async-start(f32[32,40,128]{2,1,0:T(8,128)} %shard_map.155), calls=%async_computation | async-start | bytes 1310720 | tf_op jit(solution)/shard_map/all_to_all | solution.py:275
  10.0 3.1 %shard_map.153 = (f32[32,768]{1,0:T(8,128)S(1)}, f32[32,768]{1,0:T(8,128)S(1)}) custom-call(f32[64,960]{1,0:T(8,128)} %bitcast.14, f32[960,768]{1,0:T(8,128)} %refs_2_.3, f32[960,768]{1,0:T(8,128)} %bitcast.8), custom_call_target="tpu_custom_call" | custom-call | flops 283115520 | bytes 5898240 | tf_op jit(solution)/shard_map/pallas_call | solution.py:303
  13.1 0.3 collective-permute-start
  13.4 1.1 %collective-permute-done = f32[32,768]{1,0:T(8,128)S(1)} collective-permute-done((f32[32,768]{1,0:T(8,128)S(1)}, f32[32,768]{1,0:T(8,128)S(1)}, u32[]{:S(2)}, u32[]{:S(2)}) %collective-permute-start) | collective-permute-done | bytes 98336 | tf_op jit(solution)/shard_map/ppermute | solution.py:283
  14.5 1.8 %collective-permute-start.1 = (f32[32,768]{1,0:T(8,128)S(1)}, f32[32,768]{1,0:T(8,128)S(1)}, u32[]{:S(2)}, u32[]{:S(2)}) collective-permute-start(f32[32,768]{1,0:T(8,128)S(1)} %add.15), channel_id=1, source_target_pairs={{0,16},{16,0},{1,17},{17,1},{2,18},{18,2},{3,19},{19,3},{4,20},{20... | collective-permute-start | bytes 294920 | tf_op jit(solution)/shard_map/ppermute | solution.py:279
  16.3 2.8 %shard_map.154 = (f32[16,40,128]{2,1,0:T(8,128)}, f32[16,40,128]{2,1,0:T(8,128)}) custom-call(f32[192,768]{1,0:T(8,128)} %bitcast.9, f32[192,768]{1,0:T(8,128)} %bitcast.11, f32[4,48]{1,0:T(4,128)} %refs_4_.1, f32[4,48]{1,0:T(4,128)} %refs_5_.1), custom_call_target="tpu_custom_call" | custom-call | bytes 1836544 | tf_op jit(solution)/shard_map/pallas_call | solution.py:256
  19.1 1.9 %collective-permute-done.1 = f32[32,768]{1,0:T(8,128)S(1)} collective-permute-done((f32[32,768]{1,0:T(8,128)S(1)}, f32[32,768]{1,0:T(8,128)S(1)}, u32[]{:S(2)}, u32[]{:S(2)}) %collective-permute-start.1) | collective-permute-done | bytes 98336 | tf_op jit(solution)/shard_map/ppermute | solution.py:279
  21.1 1.4 %collective-permute-start.2 = (f32[32,768]{1,0:T(8,128)S(1)}, f32[32,768]{1,0:T(8,128)S(1)}, u32[]{:S(2)}, u32[]{:S(2)}) collective-permute-start(f32[32,768]{1,0:T(8,128)S(1)} %add.16), channel_id=1, source_target_pairs={{0,4},{1,5},{2,6},{3,7},{4,0},{5,1},{6,2},{7,3},{8,12},{9,13},{10,... | collective-permute-start | bytes 294920 | tf_op jit(solution)/shard_map/ppermute | solution.py:283
  22.5 5.6 %collective-permute-done.2 = f32[32,768]{1,0:T(8,128)S(1)} collective-permute-done((f32[32,768]{1,0:T(8,128)S(1)}, f32[32,768]{1,0:T(8,128)S(1)}, u32[]{:S(2)}, u32[]{:S(2)}) %collective-permute-start.2) | collective-permute-done | bytes 98336 | tf_op jit(solution)/shard_map/ppermute | solution.py:283
  28.2 0.7 %collective-permute-start.3 = (f32[32,768]{1,0:T(8,128)S(1)}, f32[32,768]{1,0:T(8,128)S(1)}, u32[]{:S(2)}, u32[]{:S(2)}) collective-permute-start(f32[32,768]{1,0:T(8,128)S(1)} %add.17), channel_id=1, source_target_pairs={{0,8},{1,9},{2,10},{3,11},{4,12},{5,13},{6,14},{7,15},{8,0},{9,1},... | collective-permute-start | bytes 294920 | tf_op jit(solution)/shard_map/ppermute | solution.py:283
  28.8 0.0 all-to-all-done.refs_2_
  28.8 2.0 %shard_map.156 = (bf16[32,40,128]{2,1,0:T(8,128)(2,1)}, f32[16,40,128]{2,1,0:T(8,128)}) custom-call(f32[16,40,128]{2,1,0:T(8,128)} %get-tuple-element.28.refs_0_, f32[16,40,128]{2,1,0:T(8,128)} %get-tuple-element.29.refs_1_, f32[32,40,128]{2,1,0:T(8,128)S(1)} %all-to-all-done.refs_2_), custom_call_target="tpu_custom_call" | custom-call | bytes 1966080 | tf_op jit(solution)/shard_map/pallas_call | solution.py:256
  30.9 1.1 %collective-permute-start.6 = (f32[16,40,128]{2,1,0:T(8,128)}, f32[16,40,128]{2,1,0:T(8,128)S(1)}, u32[]{:S(2)}, u32[]{:S(2)}) collective-permute-start(f32[16,40,128]{2,1,0:T(8,128)} %get-tuple-element.30.refs_0_), channel_id=1, source_target_pairs={{0,16},{16,0},{1,17},{17,1},{2,18},{18,2},{3,19},{19,3},{4,20},{20... | collective-permute-start | bytes 983048 | tf_op jit(solution)/shard_map/ppermute | solution.py:279
  32.0 2.4 %collective-permute-done.3 = f32[32,768]{1,0:T(8,128)S(1)} collective-permute-done((f32[32,768]{1,0:T(8,128)S(1)}, f32[32,768]{1,0:T(8,128)S(1)}, u32[]{:S(2)}, u32[]{:S(2)}) %collective-permute-start.3) | collective-permute-done | bytes 98336 | tf_op jit(solution)/shard_map/ppermute | solution.py:283
  34.4 1.2 %collective-permute-start.4 = (f32[32,768]{1,0:T(8,128)S(1)}, f32[32,768]{1,0:T(8,128)S(1)}, u32[]{:S(2)}, u32[]{:S(2)}) collective-permute-start(f32[32,768]{1,0:T(8,128)S(1)} %add.18), channel_id=1, source_target_pairs={{0,2},{1,3},{2,0},{3,1},{4,6},{5,7},{6,4},{7,5},{8,10},{9,11},{10,... | collective-permute-start | bytes 294920 | tf_op jit(solution)/shard_map/ppermute | solution.py:283
  35.6 3.3 %all-to-all-start.1 = ((bf16[32,40,128]{2,1,0:T(8,128)(2,1)}), bf16[32,40,128]{2,1,0:T(8,128)(2,1)S(1)}, u32[]{:S(2)}, u32[]{:S(2)}) async-start(bf16[32,40,128]{2,1,0:T(8,128)(2,1)} %get-tuple-element.40), calls=%async_computation.1 | async-start | bytes 655360 | tf_op jit(solution)/shard_map/all_to_all | solution.py:275
  38.9 0.1 collective-permute-done.4
  39.1 0.2 collective-permute-start.5
  39.3 1.2 %collective-permute-done.5.other_ref = f32[32,768]{1,0:T(8,128)S(1)} collective-permute-done((f32[32,768]{1,0:T(8,128)S(1)}, f32[32,768]{1,0:T(8,128)S(1)}, u32[]{:S(2)}, u32[]{:S(2)}) %collective-permute-start.5) | collective-permute-done | bytes 98336 | tf_op jit(solution)/shard_map/ppermute | solution.py:283
  40.4 0.1 shard_map.157.refs_0_
  40.5 0.0 collective-permute-done.6.refs_1_
  40.5 2.7 %shard_map.159 = (f32[192,768]{1,0:T(8,128)}, f32[192,768]{1,0:T(8,128)}, f32[4,48]{1,0:T(4,128)}, f32[4,48]{1,0:T(4,128)}) custom-call(f32[16,40,128]{2,1,0:T(8,128)} %get-tuple-element.30.refs_0_, f32[16,40,128]{2,1,0:T(8,128)S(1)} %collective-permute-done.6.refs_1_, f32[192,768]{1,0:T(8,128)} %bitcast.10, f32[192,768]{1,0:T(8,128)} %bitcast.12, ...), custom_call_target="tpu_custom_call" | custom-call | bytes 3017728 | tf_op jit(solution)/shard_map/pallas_call | solution.py:256
  43.2 4.7 %shard_map.158 = (f32[960,768]{1,0:T(8,128)}, f32[960,768]{1,0:T(8,128)}) custom-call(bf16[192,768]{1,0:T(8,128)(2,1)S(1)} %shard_map.157.refs_0_, f32[64,960]{1,0:T(8,128)} %bitcast.15, f32[960,768]{1,0:T(8,128)} %refs_2_.3, f32[960,768]{1,0:T(8,128)} %refs_3_.3), custom_call_target="tpu_custom_call" | custom-call | flops 5096079360 | bytes 222068736 | tf_op jit(solution)/shard_map/pallas_call | solution.py:256
  48.0 2.7 %all-to-all-done.1.refs_0_ = bf16[32,40,128]{2,1,0:T(8,128)(2,1)S(1)} async-done(((bf16[32,40,128]{2,1,0:T(8,128)(2,1)}), bf16[32,40,128]{2,1,0:T(8,128)(2,1)S(1)}, u32[]{:S(2)}, u32[]{:S(2)}) %all-to-all-start.1) | async-done | bytes 327712 | tf_op jit(solution)/shard_map/all_to_all | solution.py:275
  50.6 0.9 %shard_map.160 = bf16[48,3072]{1,0:T(8,128)(2,1)} custom-call(bf16[32,40,128]{2,1,0:T(8,128)(2,1)S(1)} %all-to-all-done.1.refs_0_), custom_call_target="tpu_custom_call" | custom-call | bytes 622592 | tf_op jit(solution)/shard_map/pallas_call | solution.py:256
  (5 shorter events, 0.1 us)
Async XLA Ops:
  2.7 26.2 %all-to-all-start = ((f32[32,40,128]{2,1,0:T(8,128)}), f32[32,40,128]{2,1,0:T(8,128)S(1)}, u32[]{:S(2)}, u32[]{:S(2)}) async-start(f32[32,40,128]{2,1,0:T(8,128)} %shard_map.155), calls=%async_computation | async-start | bytes 1310720 | tf_op jit(solution)/shard_map/all_to_all | solution.py:275
  13.1 1.4 %collective-permute-start = (f32[32,768]{1,0:T(8,128)S(1)}, f32[32,768]{1,0:T(8,128)S(1)}, u32[]{:S(2)}, u32[]{:S(2)}) collective-permute-start(f32[32,768]{1,0:T(8,128)S(1)} %get-tuple-element.25), channel_id=1, source_target_pairs={{0,1},{1,0},{2,3},{3,2},{4,5},{5,4},{6,7},{7,6},{8,9},{9,8},{10,11... | collective-permute-start | bytes 294920 | tf_op jit(solution)/shard_map/ppermute | solution.py:283
  14.5 6.6 %collective-permute-start.1 = (f32[32,768]{1,0:T(8,128)S(1)}, f32[32,768]{1,0:T(8,128)S(1)}, u32[]{:S(2)}, u32[]{:S(2)}) collective-permute-start(f32[32,768]{1,0:T(8,128)S(1)} %add.15), channel_id=1, source_target_pairs={{0,16},{16,0},{1,17},{17,1},{2,18},{18,2},{3,19},{19,3},{4,20},{20... | collective-permute-start | bytes 294920 | tf_op jit(solution)/shard_map/ppermute | solution.py:279
  21.1 7.1 %collective-permute-start.2 = (f32[32,768]{1,0:T(8,128)S(1)}, f32[32,768]{1,0:T(8,128)S(1)}, u32[]{:S(2)}, u32[]{:S(2)}) collective-permute-start(f32[32,768]{1,0:T(8,128)S(1)} %add.16), channel_id=1, source_target_pairs={{0,4},{1,5},{2,6},{3,7},{4,0},{5,1},{6,2},{7,3},{8,12},{9,13},{10,... | collective-permute-start | bytes 294920 | tf_op jit(solution)/shard_map/ppermute | solution.py:283
  28.2 6.2 %collective-permute-start.3 = (f32[32,768]{1,0:T(8,128)S(1)}, f32[32,768]{1,0:T(8,128)S(1)}, u32[]{:S(2)}, u32[]{:S(2)}) collective-permute-start(f32[32,768]{1,0:T(8,128)S(1)} %add.17), channel_id=1, source_target_pairs={{0,8},{1,9},{2,10},{3,11},{4,12},{5,13},{6,14},{7,15},{8,0},{9,1},... | collective-permute-start | bytes 294920 | tf_op jit(solution)/shard_map/ppermute | solution.py:283
  30.9 9.6 %collective-permute-start.6 = (f32[16,40,128]{2,1,0:T(8,128)}, f32[16,40,128]{2,1,0:T(8,128)S(1)}, u32[]{:S(2)}, u32[]{:S(2)}) collective-permute-start(f32[16,40,128]{2,1,0:T(8,128)} %get-tuple-element.30.refs_0_), channel_id=1, source_target_pairs={{0,16},{16,0},{1,17},{17,1},{2,18},{18,2},{3,19},{19,3},{4,20},{20... | collective-permute-start | bytes 983048 | tf_op jit(solution)/shard_map/ppermute | solution.py:279
  34.4 4.7 %collective-permute-start.4 = (f32[32,768]{1,0:T(8,128)S(1)}, f32[32,768]{1,0:T(8,128)S(1)}, u32[]{:S(2)}, u32[]{:S(2)}) collective-permute-start(f32[32,768]{1,0:T(8,128)S(1)} %add.18), channel_id=1, source_target_pairs={{0,2},{1,3},{2,0},{3,1},{4,6},{5,7},{6,4},{7,5},{8,10},{9,11},{10,... | collective-permute-start | bytes 294920 | tf_op jit(solution)/shard_map/ppermute | solution.py:283
  35.6 15.0 %all-to-all-start.1 = ((bf16[32,40,128]{2,1,0:T(8,128)(2,1)}), bf16[32,40,128]{2,1,0:T(8,128)(2,1)S(1)}, u32[]{:S(2)}, u32[]{:S(2)}) async-start(bf16[32,40,128]{2,1,0:T(8,128)(2,1)} %get-tuple-element.40), calls=%async_computation.1 | async-start | bytes 655360 | tf_op jit(solution)/shard_map/all_to_all | solution.py:275
  39.1 1.4 %collective-permute-start.5 = (f32[32,768]{1,0:T(8,128)S(1)}, f32[32,768]{1,0:T(8,128)S(1)}, u32[]{:S(2)}, u32[]{:S(2)}) collective-permute-start(f32[32,768]{1,0:T(8,128)S(1)} %add.19.mine_ref), channel_id=1, source_target_pairs={{0,1},{1,0},{2,3},{3,2},{4,5},{5,4},{6,7},{7,6},{8,9},{9,8},{10,11... | collective-permute-start | bytes 294920 | tf_op jit(solution)/shard_map/ppermute | solution.py:283

commit v3 on v2

--- a/solution.py
+++ b/solution.py
@@ -106,9 +106,24 @@
     return jnp.concatenate([piece[24:32], roll_half(piece[24:32]), piece[32:40]], axis=0)
 
 
-def pack_kernel(shards, load, store, x_ref, norm_ref, out_ref, scr):
-    load(1)
-    tile = norm_tile(scr, norm_ref)
+def put_dense(out_ref, at, main, half):
+    mask = left_half((4, LANES))
+    for k in range(6):
+        out_ref[at, :, LANES * k : LANES * k + LANES] = main[4 * k : 4 * k + 4]
+    turned = roll_half(half)
+    for k in range(3):
+        group = jnp.where(mask, half[8 * k : 8 * k + 4], turned[8 * k + 4 : 8 * k + 8])
+        out_ref[at, :, LANES * (6 + k) : LANES * (7 + k)] = group
+
+
+def get_dense(ref, at):
+    groups = [ref[at, :, LANES * k : LANES * k + LANES] for k in range(9)]
+    tiles = [jnp.concatenate([g, roll_half(g)], axis=0) for g in groups[6:]]
+    third = jnp.where(left_half((8, LANES)), tiles[0], roll_half(tiles[1]))
+    return jnp.concatenate(groups[:6] + [third, tiles[2]], axis=0)
+
+
+def pack_kernel(shards, load, store, x_ref, out_ref):
     mask = left_half((24, LANES))
     for group in range(2):
         load(0, group)
@@ -117,16 +132,14 @@
             at = group * shards + 2 * pair
             t = [x_ref[rows, 384 * pair + LANES * k : 384 * pair + LANES * k + LANES] for k in range(3)]
             t1, t2 = roll_half(t[1]), roll_half(t[2])
-            put_piece(out_ref, at, t[0], t[1], tile)
-            put_piece(out_ref, at + 1, jnp.where(mask, t1, t2), t2, tile)
+            put_dense(out_ref, at, t[0], t[1])
+            put_dense(out_ref, at + 1, jnp.where(mask, t1, t2), t2)
         store(0, slice(group * shards, group * shards + shards))
 
 
-def states_kernel(shards, load, store, outer_ref, moment_ref, outer_norm_ref, moment_norm_ref, outer_out, moment_out, scr, tile_scr):
+def states_kernel(shards, load, store, outer_ref, moment_ref, outer_out, moment_out, scr):
     group = lax.axis_index("group")
-    for n, (src, norm, out) in enumerate(((outer_ref, outer_norm_ref, outer_out), (moment_ref, moment_norm_ref, moment_out))):
-        load(2 + n)
-        tile = norm_tile(tile_scr, norm)
+    for n, (src, out) in enumerate(((outer_ref, outer_out), (moment_ref, moment_out))):
         load(n)
         for k in range(src.shape[1] // LANES):
             cols = slice(LANES * k, LANES * k + LANES)
@@ -134,17 +147,21 @@
             scr[n, cols, LANES : LANES + HALF] = src[LANES : LANES + HALF, cols].T
         for s in range(shards):
             rows = pl.ds(pl.multiple_of(48 * s + 24 * group, 8), 24)
-            out[s] = make_piece(scr[n, rows, :LANES], scr[n, rows, LANES:], tile)
+            half = scr[n, rows, LANES:]
+            out[s] = make_piece(scr[n, rows, :LANES], half, half[16:24])
         store(n)
 
 
-def middle_kernel(shards, load, store, outer_ref, moment_ref, got_ref, send_ref, delta_ref):
-    for n in range(3):
+def middle_kernel(shards, load, store, outer_ref, moment_ref, norm_ref, got_ref, send_ref, delta_ref, scr):
+    for n in (2, 0, 1):
         load(n)
+    tile = norm_tile(scr, norm_ref)
+    mask = left_half((8, LANES))
     for s in range(shards):
         outer = outer_ref[s]
-        delta = ((outer - got_ref[s]) + (outer - got_ref[shards + s])) * 0.5
-        delta_ref[s] = delta
+        delta = ((outer - get_dense(got_ref, s)) + (outer - get_dense(got_ref, shards + s))) * 0.5
+        delta_ref[s, 0:32] = delta[0:32]
+        delta_ref[s, 32:40] = jnp.where(mask, delta[32:40], tile)
         new = nesterov(outer, moment_ref[s], delta)[0].astype(bf16)
         send_ref[s] = new
         send_ref[shards + s] = new
@@ -195,7 +212,7 @@
     shards, load, store, mine_ref, other_ref, outer_ref, moment_ref, outer_norm_ref, moment_norm_ref,
     new_ref, new_moment_ref, new_norm_ref, new_moment_norm_ref, scr,
 ):
-    group, me = lax.axis_index("group"), lax.axis_index("shard")
+    group = lax.axis_index("group")
     for n, (src, owner) in enumerate(((mine_ref, group), (other_ref, 1 - group))):
         load(n)
         for s in range(shards):
@@ -211,11 +228,11 @@
             new_ref[rows, cols], new_moment_ref[rows, cols] = nesterov(outer_ref[rows, cols], moment_ref[rows, cols], part)
     store(0)
     store(1)
-    tile = roll_half(mine_ref[me, 32:40, :])
     norms, width = outer_norm_ref.shape
-    new_norm_ref[...], new_moment_norm_ref[...] = nesterov(
-        outer_norm_ref[...], moment_norm_ref[...], tile[:norms, :width]
-    )
+    outer = outer_norm_ref[...]
+    mine, other = (roll_half(ref[0, 32:40, :])[:norms, :width] for ref in (mine_ref, other_ref))
+    delta = ((outer - mine) + (outer - other)) * 0.5
+    new_norm_ref[...], new_moment_norm_ref[...] = nesterov(outer, moment_norm_ref[...], delta)
     store(2)
     store(3)
 
@@ -295,8 +312,8 @@
     piece = (shards, ROWS, LANES)
 
     (sent,) = call(
-        functools.partial(pack_kernel, shards), (inner_attn[0], inner_norms[0]), [((2 * shards, ROWS, LANES), f32)],
-        [pltpu.VMEM((8, LANES), f32)], parts={0: [(0, 24), (24, 24)]},
+        functools.partial(pack_kernel, shards), (inner_attn[0],), [((2 * shards, 4, 9 * LANES), f32)],
+        parts={0: [(0, 24), (24, 24)]},
     )
     got = everyone(sent)
 
@@ -313,18 +330,18 @@
     )(*[pltpu.with_memory_space_constraint(x, pltpu.HBM) for x in (basis, outer_embed, inner_embed[0])])
     mine = mine + swap_shards(other, 1)
     outer_piece, moment_piece = call(
-        functools.partial(states_kernel, shards), (outer_attn, moment_attn, outer_norms, moment_norms), [(piece, f32)] * 2,
-        [pltpu.VMEM((2, outer_attn.shape[1], 2 * LANES), f32), pltpu.VMEM((8, LANES), f32)],
+        functools.partial(states_kernel, shards), (outer_attn, moment_attn), [(piece, f32)] * 2,
+        [pltpu.VMEM((2, outer_attn.shape[1], 2 * LANES), f32)],
     )
     steps = []
-    for n, step in enumerate(("x", 4, 8, 2)):
+    for n, step in enumerate(("x", 2, 4, 8)):
         moved = swap_groups(mine) if step == "x" else swap_shards(mine, step)
         if n == 0:
             moved = after(moved, outer_piece)
         if n == 2:
             send, delta = call(
-                functools.partial(middle_kernel, shards), (after(outer_piece, steps[1]), moment_piece, got),
-                [((2 * shards, ROWS, LANES), bf16), (piece, f32)], here=(2,),
+                functools.partial(middle_kernel, shards), (after(outer_piece, steps[1]), moment_piece, inner_norms[0], got),
+                [((2 * shards, ROWS, LANES), bf16), (piece, f32)], [pltpu.VMEM((8, LANES), f32)], here=(3,),
             )
             moved = after(moved, delta)
         mine = mine + moved

time: 51.8 us -> 49.4 us (0.954)
  waiting for transfers between devices: 15 us -> 9.97 us
  starting transfers between devices: 17.4 us -> 19.9 us
    ppermute x5, waiting for transfers between devices: 10.3 us -> 7.47 us  [swap_shards(): lax.ppermute(x, 'shard', [(i, i ^ bit) for i in range(lax.axis_size('shar...]
    ppermute x5, starting transfers between devices: 3.86 us -> 6.63 us  [swap_shards(): lax.ppermute(x, 'shard', [(i, i ^ bit) for i in range(lax.axis_size('shar...]
    all_to_all x2, waiting for transfers between devices: 2.67 us -> 0.85 us  [everyone(): lax.all_to_all(x, ('group', 'shard'), split_axis=0, concat_axis=0, tiled=...]
    all_to_all x2, starting transfers between devices: 10.6 us -> 9.9 us  [everyone(): lax.all_to_all(x, ('group', 'shard'), split_axis=0, concat_axis=0, tiled=...]
  transfers between devices with their start and end apart: 9 -> 9, of which waited for: 7 -> 6; matrix products, arithmetic and copies ran while one was open for 0% -> 0% of each run, Pallas kernels for 30% -> 31%
where the time goes in v3:
time: 49.4 us; the launch traced here: 49.1 us
  starting transfers between devices  19.9 us (40%)
  Pallas kernels  18.4 us (37%)
  waiting for transfers between devices  9.97 us (20%)
  between operations  0.74 us (1%)
    pallas_call x6, Pallas kernels, call(): pl.pallas_call(functools.partial(staged, kernel, parts, len(args) + len(o...  15.2 us
    all_to_all x2, starting transfers between devices, everyone(): lax.all_to_all(x, ('group', 'shard'), split_axis=0, concat_axis=0, tiled=...  9.9 us
    ppermute x5, waiting for transfers between devices, swap_shards(): lax.ppermute(x, 'shard', [(i, i ^ bit) for i in range(lax.axis_size('shar...  7.47 us
    ppermute x5, starting transfers between devices, swap_shards(): lax.ppermute(x, 'shard', [(i, i ^ bit) for i in range(lax.axis_size('shar...  6.63 us
    ppermute x2, starting transfers between devices, swap_groups(): return lax.ppermute(x, 'group', [(0, 1), (1, 0)])  3.39 us
    pallas_call x1, Pallas kernels, fast(): pl.pallas_call(coeff_kernel, out_shape=[jax.ShapeDtypeStruct((rank // 2,...  3.1 us
    ppermute x2, waiting for transfers between devices, swap_groups(): return lax.ppermute(x, 'group', [(0, 1), (1, 0)])  1.66 us
  transfers between devices with their start and end apart: 9, of which 6 were waited for; matrix products, arithmetic and copies ran while one was open for 0% of the time, Pallas kernels for 31%

profile of v3, /device:TPU:0, one launch (start us, length us, event | category | flops | bytes accessed | tf_op | source)
XLA Modules:
  0.0 49.1 jit_solution(10872490516484774852)
XLA Ops:
  0.6 2.0 %shard_map.155 = f32[32,4,1152]{2,1,0:T(4,128)} custom-call(f32[48,3072]{1,0:T(8,128)} %bitcast.13), custom_call_target="tpu_custom_call" | custom-call | bytes 1179648 | tf_op jit(solution)/shard_map/pallas_call | solution.py:273
  2.7 7.3 %all-to-all-start = ((f32[32,4,1152]{2,1,0:T(4,128)}), f32[32,4,1152]{2,1,0:T(4,128)S(1)}, u32[]{:S(2)}, u32[]{:S(2)}) async-start(f32[32,4,1152]{2,1,0:T(4,128)} %shard_map.155), calls=%async_computation | async-start | bytes 1179648 | tf_op jit(solution)/shard_map/all_to_all | solution.py:292
  10.0 3.1 %shard_map.153 = (f32[32,768]{1,0:T(8,128)S(1)}, f32[32,768]{1,0:T(8,128)S(1)}) custom-call(f32[64,960]{1,0:T(8,128)} %bitcast.14, f32[960,768]{1,0:T(8,128)} %refs_2_.1, f32[960,768]{1,0:T(8,128)} %bitcast.8), custom_call_target="tpu_custom_call" | custom-call | flops 283115520 | bytes 5898240 | tf_op jit(solution)/shard_map/pallas_call | solution.py:320
  13.1 0.3 collective-permute-start
  13.4 1.1 %collective-permute-done = f32[32,768]{1,0:T(8,128)S(1)} collective-permute-done((f32[32,768]{1,0:T(8,128)S(1)}, f32[32,768]{1,0:T(8,128)S(1)}, u32[]{:S(2)}, u32[]{:S(2)}) %collective-permute-start) | collective-permute-done | bytes 98336 | tf_op jit(solution)/shard_map/ppermute | solution.py:300
  14.5 1.8 %collective-permute-start.1 = (f32[32,768]{1,0:T(8,128)S(1)}, f32[32,768]{1,0:T(8,128)S(1)}, u32[]{:S(2)}, u32[]{:S(2)}) collective-permute-start(f32[32,768]{1,0:T(8,128)S(1)} %add.15), channel_id=1, source_target_pairs={{0,16},{16,0},{1,17},{17,1},{2,18},{18,2},{3,19},{19,3},{4,20},{20... | collective-permute-start | bytes 294920 | tf_op jit(solution)/shard_map/ppermute | solution.py:296
  16.3 2.6 %shard_map.154 = (f32[16,40,128]{2,1,0:T(8,128)}, f32[16,40,128]{2,1,0:T(8,128)}) custom-call(f32[192,768]{1,0:T(8,128)} %bitcast.9, f32[192,768]{1,0:T(8,128)} %bitcast.11), custom_call_target="tpu_custom_call" | custom-call | bytes 1835008 | tf_op jit(solution)/shard_map/pallas_call | solution.py:273
  19.0 1.7 %collective-permute-done.1 = f32[32,768]{1,0:T(8,128)S(1)} collective-permute-done((f32[32,768]{1,0:T(8,128)S(1)}, f32[32,768]{1,0:T(8,128)S(1)}, u32[]{:S(2)}, u32[]{:S(2)}) %collective-permute-start.1) | collective-permute-done | bytes 98336 | tf_op jit(solution)/shard_map/ppermute | solution.py:296
  20.6 1.6 %collective-permute-start.2 = (f32[32,768]{1,0:T(8,128)S(1)}, f32[32,768]{1,0:T(8,128)S(1)}, u32[]{:S(2)}, u32[]{:S(2)}) collective-permute-start(f32[32,768]{1,0:T(8,128)S(1)} %add.16), channel_id=1, source_target_pairs={{0,2},{1,3},{2,0},{3,1},{4,6},{5,7},{6,4},{7,5},{8,10},{9,11},{10,... | collective-permute-start | bytes 294920 | tf_op jit(solution)/shard_map/ppermute | solution.py:300
  22.3 3.2 %collective-permute-done.2 = f32[32,768]{1,0:T(8,128)S(1)} collective-permute-done((f32[32,768]{1,0:T(8,128)S(1)}, f32[32,768]{1,0:T(8,128)S(1)}, u32[]{:S(2)}, u32[]{:S(2)}) %collective-permute-start.2) | collective-permute-done | bytes 98336 | tf_op jit(solution)/shard_map/ppermute | solution.py:300
  25.5 2.6 %collective-permute-start.3 = (f32[32,768]{1,0:T(8,128)S(1)}, f32[32,768]{1,0:T(8,128)S(1)}, u32[]{:S(2)}, u32[]{:S(2)}) collective-permute-start(f32[32,768]{1,0:T(8,128)S(1)} %add.17), channel_id=1, source_target_pairs={{0,4},{1,5},{2,6},{3,7},{4,0},{5,1},{6,2},{7,3},{8,12},{9,13},{10,... | collective-permute-start | bytes 294920 | tf_op jit(solution)/shard_map/ppermute | solution.py:300
  28.0 0.0 all-to-all-done.refs_3_
  28.0 2.2 %shard_map.156 = (bf16[32,40,128]{2,1,0:T(8,128)(2,1)}, f32[16,40,128]{2,1,0:T(8,128)}) custom-call(f32[16,40,128]{2,1,0:T(8,128)} %get-tuple-element.28.refs_0_, f32[16,40,128]{2,1,0:T(8,128)} %get-tuple-element.29.refs_1_, f32[4,48]{1,0:T(4,128)} %bitcast.16, f32[32,4,1152]{2,1,0:T(4,128)S(1)} %all-to-all-done.refs_3_), custom_call_target="tpu_custom_call" | custom-call | bytes 1901312 | tf_op jit(solution)/shard_map/pallas_call | solution.py:273
  30.2 1.6 %collective-permute-start.6 = (f32[16,40,128]{2,1,0:T(8,128)}, f32[16,40,128]{2,1,0:T(8,128)S(1)}, u32[]{:S(2)}, u32[]{:S(2)}) collective-permute-start(f32[16,40,128]{2,1,0:T(8,128)} %get-tuple-element.30.refs_0_), channel_id=1, source_target_pairs={{0,16},{16,0},{1,17},{17,1},{2,18},{18,2},{3,19},{19,3},{4,20},{20... | collective-permute-start | bytes 983048 | tf_op jit(solution)/shard_map/ppermute | solution.py:296
  31.8 0.0 collective-permute-done.3
  31.8 2.1 %collective-permute-start.4 = (f32[32,768]{1,0:T(8,128)S(1)}, f32[32,768]{1,0:T(8,128)S(1)}, u32[]{:S(2)}, u32[]{:S(2)}) collective-permute-start(f32[32,768]{1,0:T(8,128)S(1)} %add.18), channel_id=1, source_target_pairs={{0,8},{1,9},{2,10},{3,11},{4,12},{5,13},{6,14},{7,15},{8,0},{9,1},... | collective-permute-start | bytes 294920 | tf_op jit(solution)/shard_map/ppermute | solution.py:300
  33.9 2.6 %all-to-all-start.1 = ((bf16[32,40,128]{2,1,0:T(8,128)(2,1)}), bf16[32,40,128]{2,1,0:T(8,128)(2,1)S(1)}, u32[]{:S(2)}, u32[]{:S(2)}) async-start(bf16[32,40,128]{2,1,0:T(8,128)(2,1)} %get-tuple-element.40), calls=%async_computation.1 | async-start | bytes 655360 | tf_op jit(solution)/shard_map/all_to_all | solution.py:292
  36.5 2.0 %collective-permute-done.4 = f32[32,768]{1,0:T(8,128)S(1)} collective-permute-done((f32[32,768]{1,0:T(8,128)S(1)}, f32[32,768]{1,0:T(8,128)S(1)}, u32[]{:S(2)}, u32[]{:S(2)}) %collective-permute-start.4) | collective-permute-done | bytes 98336 | tf_op jit(solution)/shard_map/ppermute | solution.py:300
  38.5 0.1 collective-permute-start.5
  38.6 1.3 %collective-permute-done.5.other_ref = f32[32,768]{1,0:T(8,128)S(1)} collective-permute-done((f32[32,768]{1,0:T(8,128)S(1)}, f32[32,768]{1,0:T(8,128)S(1)}, u32[]{:S(2)}, u32[]{:S(2)}) %collective-permute-start.5) | collective-permute-done | bytes 98336 | tf_op jit(solution)/shard_map/ppermute | solution.py:300
  39.8 0.1 shard_map.157.refs_0_
  39.9 0.0 collective-permute-done.6.refs_1_
  39.9 2.7 %shard_map.159 = (f32[192,768]{1,0:T(8,128)}, f32[192,768]{1,0:T(8,128)}, f32[4,48]{1,0:T(4,128)}, f32[4,48]{1,0:T(4,128)}) custom-call(f32[16,40,128]{2,1,0:T(8,128)} %get-tuple-element.30.refs_0_, f32[16,40,128]{2,1,0:T(8,128)S(1)} %collective-permute-done.6.refs_1_, f32[192,768]{1,0:T(8,128)} %bitcast.10, f32[192,768]{1,0:T(8,128)} %bitcast.12, ...), custom_call_target="tpu_custom_call" | custom-call | bytes 3017728 | tf_op jit(solution)/shard_map/pallas_call | solution.py:273
  42.6 4.7 %shard_map.158 = (f32[960,768]{1,0:T(8,128)}, f32[960,768]{1,0:T(8,128)}) custom-call(bf16[192,768]{1,0:T(8,128)(2,1)S(1)} %shard_map.157.refs_0_, f32[64,960]{1,0:T(8,128)} %bitcast.15, f32[960,768]{1,0:T(8,128)} %refs_2_.1, f32[960,768]{1,0:T(8,128)} %refs_3_.1), custom_call_target="tpu_custom_call" | custom-call | flops 5096079360 | bytes 222068736 | tf_op jit(solution)/shard_map/pallas_call | solution.py:273
  47.3 0.8 %all-to-all-done.1.refs_0_ = bf16[32,40,128]{2,1,0:T(8,128)(2,1)S(1)} async-done(((bf16[32,40,128]{2,1,0:T(8,128)(2,1)}), bf16[32,40,128]{2,1,0:T(8,128)(2,1)S(1)}, u32[]{:S(2)}, u32[]{:S(2)}) %all-to-all-start.1) | async-done | bytes 327712 | tf_op jit(solution)/shard_map/all_to_all | solution.py:292
  48.2 0.9 %shard_map.160 = bf16[48,3072]{1,0:T(8,128)(2,1)} custom-call(bf16[32,40,128]{2,1,0:T(8,128)(2,1)S(1)} %all-to-all-done.1.refs_0_), custom_call_target="tpu_custom_call" | custom-call | bytes 622592 | tf_op jit(solution)/shard_map/pallas_call | solution.py:273
  (5 shorter events, 0.1 us)
Async XLA Ops:
  2.7 25.3 %all-to-all-start = ((f32[32,4,1152]{2,1,0:T(4,128)}), f32[32,4,1152]{2,1,0:T(4,128)S(1)}, u32[]{:S(2)}, u32[]{:S(2)}) async-start(f32[32,4,1152]{2,1,0:T(4,128)} %shard_map.155), calls=%async_computation | async-start | bytes 1179648 | tf_op jit(solution)/shard_map/all_to_all | solution.py:292
  13.1 1.4 %collective-permute-start = (f32[32,768]{1,0:T(8,128)S(1)}, f32[32,768]{1,0:T(8,128)S(1)}, u32[]{:S(2)}, u32[]{:S(2)}) collective-permute-start(f32[32,768]{1,0:T(8,128)S(1)} %get-tuple-element.25), channel_id=1, source_target_pairs={{0,1},{1,0},{2,3},{3,2},{4,5},{5,4},{6,7},{7,6},{8,9},{9,8},{10,11... | collective-permute-start | bytes 294920 | tf_op jit(solution)/shard_map/ppermute | solution.py:300
  14.5 6.1 %collective-permute-start.1 = (f32[32,768]{1,0:T(8,128)S(1)}, f32[32,768]{1,0:T(8,128)S(1)}, u32[]{:S(2)}, u32[]{:S(2)}) collective-permute-start(f32[32,768]{1,0:T(8,128)S(1)} %add.15), channel_id=1, source_target_pairs={{0,16},{16,0},{1,17},{17,1},{2,18},{18,2},{3,19},{19,3},{4,20},{20... | collective-permute-start | bytes 294920 | tf_op jit(solution)/shard_map/ppermute | solution.py:296
  20.6 4.8 %collective-permute-start.2 = (f32[32,768]{1,0:T(8,128)S(1)}, f32[32,768]{1,0:T(8,128)S(1)}, u32[]{:S(2)}, u32[]{:S(2)}) collective-permute-start(f32[32,768]{1,0:T(8,128)S(1)} %add.16), channel_id=1, source_target_pairs={{0,2},{1,3},{2,0},{3,1},{4,6},{5,7},{6,4},{7,5},{8,10},{9,11},{10,... | collective-permute-start | bytes 294920 | tf_op jit(solution)/shard_map/ppermute | solution.py:300
  25.5 6.4 %collective-permute-start.3 = (f32[32,768]{1,0:T(8,128)S(1)}, f32[32,768]{1,0:T(8,128)S(1)}, u32[]{:S(2)}, u32[]{:S(2)}) collective-permute-start(f32[32,768]{1,0:T(8,128)S(1)} %add.17), channel_id=1, source_target_pairs={{0,4},{1,5},{2,6},{3,7},{4,0},{5,1},{6,2},{7,3},{8,12},{9,13},{10,... | collective-permute-start | bytes 294920 | tf_op jit(solution)/shard_map/ppermute | solution.py:300
  30.2 9.7 %collective-permute-start.6 = (f32[16,40,128]{2,1,0:T(8,128)}, f32[16,40,128]{2,1,0:T(8,128)S(1)}, u32[]{:S(2)}, u32[]{:S(2)}) collective-permute-start(f32[16,40,128]{2,1,0:T(8,128)} %get-tuple-element.30.refs_0_), channel_id=1, source_target_pairs={{0,16},{16,0},{1,17},{17,1},{2,18},{18,2},{3,19},{19,3},{4,20},{20... | collective-permute-start | bytes 983048 | tf_op jit(solution)/shard_map/ppermute | solution.py:296
  31.8 6.6 %collective-permute-start.4 = (f32[32,768]{1,0:T(8,128)S(1)}, f32[32,768]{1,0:T(8,128)S(1)}, u32[]{:S(2)}, u32[]{:S(2)}) collective-permute-start(f32[32,768]{1,0:T(8,128)S(1)} %add.18), channel_id=1, source_target_pairs={{0,8},{1,9},{2,10},{3,11},{4,12},{5,13},{6,14},{7,15},{8,0},{9,1},... | collective-permute-start | bytes 294920 | tf_op jit(solution)/shard_map/ppermute | solution.py:300
  33.9 14.3 %all-to-all-start.1 = ((bf16[32,40,128]{2,1,0:T(8,128)(2,1)}), bf16[32,40,128]{2,1,0:T(8,128)(2,1)S(1)}, u32[]{:S(2)}, u32[]{:S(2)}) async-start(bf16[32,40,128]{2,1,0:T(8,128)(2,1)} %get-tuple-element.40), calls=%async_computation.1 | async-start | bytes 655360 | tf_op jit(solution)/shard_map/all_to_all | solution.py:292
  38.5 1.4 %collective-permute-start.5 = (f32[32,768]{1,0:T(8,128)S(1)}, f32[32,768]{1,0:T(8,128)S(1)}, u32[]{:S(2)}, u32[]{:S(2)}) collective-permute-start(f32[32,768]{1,0:T(8,128)S(1)} %add.19.mine_ref), channel_id=1, source_target_pairs={{0,1},{1,0},{2,3},{3,2},{4,5},{5,4},{6,7},{7,6},{8,9},{9,8},{10,11... | collective-permute-start | bytes 294920 | tf_op jit(solution)/shard_map/ppermute | solution.py:300

commit v4 on v3

--- a/solution.py
+++ b/solution.py
@@ -300,6 +300,21 @@
     return lax.ppermute(x, "shard", [(i, i ^ bit) for i in range(lax.axis_size("shard"))])
 
 
+def hop(x, *masks):
+    devices = lax.axis_size("group") * lax.axis_size("shard")
+    return lax.ppermute(x, ("group", "shard"), [(d, d ^ masks[d % 2]) for d in range(devices)])
+
+
+def hops(shards):
+    bits = [shards]
+    while len(bits) == 1 or 2 * bits[-1] < shards:
+        bits.append(2 * bits[-1] if len(bits) > 1 else 2)
+    order = []
+    for a, b in zip(bits[::2], bits[1::2]):
+        order += [(a, b), (b, a)]
+    return order + ([(bits[-1],) * 2] if len(bits) % 2 else [])
+
+
 def fast(
     inner_embed, outer_embed, moment_embed, basis, inner_attn, outer_attn, moment_attn,
     inner_norms, outer_norms, moment_norms,
@@ -334,8 +349,8 @@
         [pltpu.VMEM((2, outer_attn.shape[1], 2 * LANES), f32)],
     )
     steps = []
-    for n, step in enumerate(("x", 2, 4, 8)):
-        moved = swap_groups(mine) if step == "x" else swap_shards(mine, step)
+    for n, masks in enumerate(hops(shards)):
+        moved = hop(mine, *masks)
         if n == 0:
             moved = after(moved, outer_piece)
         if n == 2:

time: 49.4 us -> 48.9 us (0.990)
  starting transfers between devices: 19.9 us -> 19.4 us
    ppermute x0 -> x4, starting transfers between devices: none -> 7.4 us  [hop(): lax.ppermute(x, ('group', 'shard'), [(d, d ^ masks[d % 2]) for d in range...]
    ppermute x5 -> x2, starting transfers between devices: 6.63 us -> 0.39 us  [swap_shards(): lax.ppermute(x, 'shard', [(i, i ^ bit) for i in range(lax.axis_size('shar...]
    ppermute x0 -> x4, waiting for transfers between devices: none -> 5.25 us  [hop(): lax.ppermute(x, ('group', 'shard'), [(d, d ^ masks[d % 2]) for d in range...]
    ppermute x5 -> x2, waiting for transfers between devices: 7.47 us -> 2.34 us  [swap_shards(): lax.ppermute(x, 'shard', [(i, i ^ bit) for i in range(lax.axis_size('shar...]
    ppermute x2 -> x1, starting transfers between devices: 3.39 us -> 1.08 us  [swap_groups(): return lax.ppermute(x, 'group', [(0, 1), (1, 0)])]
    ppermute x2 -> x1, waiting for transfers between devices: 1.66 us -> 0.48 us  [swap_groups(): return lax.ppermute(x, 'group', [(0, 1), (1, 0)])]
    all_to_all x2, waiting for transfers between devices: 0.85 us -> 1.92 us  [everyone(): lax.all_to_all(x, ('group', 'shard'), split_axis=0, concat_axis=0, tiled=...]
    all_to_all x2, starting transfers between devices: 9.9 us -> 10.6 us  [everyone(): lax.all_to_all(x, ('group', 'shard'), split_axis=0, concat_axis=0, tiled=...]
  transfers between devices with their start and end apart: 9 -> 9, of which waited for: 6 -> 8; matrix products, arithmetic and copies ran while one was open for 0% -> 0% of each run, Pallas kernels for 31% -> 32%
where the time goes in v4:
time: 48.9 us; the launch traced here: 48.6 us
  starting transfers between devices  19.4 us (40%)
  Pallas kernels  18.4 us (38%)
  waiting for transfers between devices  9.99 us (20%)
  between operations  0.74 us (2%)
    pallas_call x6, Pallas kernels, call(): pl.pallas_call(functools.partial(staged, kernel, parts, len(args) + len(o...  15.2 us
    all_to_all x2, starting transfers between devices, everyone(): lax.all_to_all(x, ('group', 'shard'), split_axis=0, concat_axis=0, tiled=...  10.6 us
    ppermute x4, starting transfers between devices, hop(): lax.ppermute(x, ('group', 'shard'), [(d, d ^ masks[d % 2]) for d in range...  7.4 us
    ppermute x4, waiting for transfers between devices, hop(): lax.ppermute(x, ('group', 'shard'), [(d, d ^ masks[d % 2]) for d in range...  5.25 us
    pallas_call x1, Pallas kernels, fast(): pl.pallas_call(coeff_kernel, out_shape=[jax.ShapeDtypeStruct((rank // 2,...  3.1 us
    ppermute x2, waiting for transfers between devices, swap_shards(): lax.ppermute(x, 'shard', [(i, i ^ bit) for i in range(lax.axis_size('shar...  2.34 us
    all_to_all x2, waiting for transfers between devices, everyone(): lax.all_to_all(x, ('group', 'shard'), split_axis=0, concat_axis=0, tiled=...  1.92 us
    ppermute x1, starting transfers between devices, swap_groups(): return lax.ppermute(x, 'group', [(0, 1), (1, 0)])  1.08 us
  transfers between devices with their start and end apart: 9, of which 8 were waited for; matrix products, arithmetic and copies ran while one was open for 0% of the time, Pallas kernels for 32%

profile of v4, /device:TPU:0, one launch (start us, length us, event | category | flops | bytes accessed | tf_op | source)
XLA Modules:
  0.0 48.6 jit_solution(4658907378030850304)
XLA Ops:
  0.6 2.0 %shard_map.155 = f32[32,4,1152]{2,1,0:T(4,128)} custom-call(f32[48,3072]{1,0:T(8,128)} %bitcast.13), custom_call_target="tpu_custom_call" | custom-call | bytes 1179648 | tf_op jit(solution)/shard_map/pallas_call | solution.py:273
  2.7 7.3 %all-to-all-start = ((f32[32,4,1152]{2,1,0:T(4,128)}), f32[32,4,1152]{2,1,0:T(4,128)S(1)}, u32[]{:S(2)}, u32[]{:S(2)}) async-start(f32[32,4,1152]{2,1,0:T(4,128)} %shard_map.155), calls=%async_computation | async-start | bytes 1179648 | tf_op jit(solution)/shard_map/all_to_all | solution.py:292
  10.0 3.1 %shard_map.153 = (f32[32,768]{1,0:T(8,128)S(1)}, f32[32,768]{1,0:T(8,128)S(1)}) custom-call(f32[64,960]{1,0:T(8,128)} %bitcast.14, f32[960,768]{1,0:T(8,128)} %refs_2_.1, f32[960,768]{1,0:T(8,128)} %bitcast.8), custom_call_target="tpu_custom_call" | custom-call | flops 283115520 | bytes 5898240 | tf_op jit(solution)/shard_map/pallas_call | solution.py:335
  13.1 0.3 collective-permute-start
  13.4 1.1 %collective-permute-done = f32[32,768]{1,0:T(8,128)S(1)} collective-permute-done((f32[32,768]{1,0:T(8,128)S(1)}, f32[32,768]{1,0:T(8,128)S(1)}, u32[]{:S(2)}, u32[]{:S(2)}) %collective-permute-start) | collective-permute-done | bytes 98336 | tf_op jit(solution)/shard_map/ppermute | solution.py:300
  14.5 1.8 %collective-permute-start.1 = (f32[32,768]{1,0:T(8,128)S(1)}, f32[32,768]{1,0:T(8,128)S(1)}, u32[]{:S(2)}, u32[]{:S(2)}) collective-permute-start(f32[32,768]{1,0:T(8,128)S(1)} %add.15), channel_id=1, source_target_pairs={{0,16},{1,3},{2,18},{3,1},{4,20},{5,7},{6,22},{7,5},{8,24},{9,11},... | collective-permute-start | bytes 294920 | tf_op jit(solution)/shard_map/ppermute | solution.py:305
  16.3 2.6 %shard_map.154 = (f32[16,40,128]{2,1,0:T(8,128)}, f32[16,40,128]{2,1,0:T(8,128)}) custom-call(f32[192,768]{1,0:T(8,128)} %bitcast.9, f32[192,768]{1,0:T(8,128)} %bitcast.11), custom_call_target="tpu_custom_call" | custom-call | bytes 1835008 | tf_op jit(solution)/shard_map/pallas_call | solution.py:273
  19.0 0.9 %collective-permute-done.1 = f32[32,768]{1,0:T(8,128)S(1)} collective-permute-done((f32[32,768]{1,0:T(8,128)S(1)}, f32[32,768]{1,0:T(8,128)S(1)}, u32[]{:S(2)}, u32[]{:S(2)}) %collective-permute-start.1) | collective-permute-done | bytes 98336 | tf_op jit(solution)/shard_map/ppermute | solution.py:305
  19.9 1.6 %collective-permute-start.2 = (f32[32,768]{1,0:T(8,128)S(1)}, f32[32,768]{1,0:T(8,128)S(1)}, u32[]{:S(2)}, u32[]{:S(2)}) collective-permute-start(f32[32,768]{1,0:T(8,128)S(1)} %add.16), channel_id=1, source_target_pairs={{0,2},{1,17},{2,0},{3,19},{4,6},{5,21},{6,4},{7,23},{8,10},{9,25},... | collective-permute-start | bytes 294920 | tf_op jit(solution)/shard_map/ppermute | solution.py:305
  21.5 3.1 %collective-permute-done.2 = f32[32,768]{1,0:T(8,128)S(1)} collective-permute-done((f32[32,768]{1,0:T(8,128)S(1)}, f32[32,768]{1,0:T(8,128)S(1)}, u32[]{:S(2)}, u32[]{:S(2)}) %collective-permute-start.2) | collective-permute-done | bytes 98336 | tf_op jit(solution)/shard_map/ppermute | solution.py:305
  24.6 1.8 %collective-permute-start.3 = (f32[32,768]{1,0:T(8,128)S(1)}, f32[32,768]{1,0:T(8,128)S(1)}, u32[]{:S(2)}, u32[]{:S(2)}) collective-permute-start(f32[32,768]{1,0:T(8,128)S(1)} %add.17), channel_id=1, source_target_pairs={{0,4},{1,9},{2,6},{3,11},{4,0},{5,13},{6,2},{7,15},{8,12},{9,1},{1... | collective-permute-start | bytes 294920 | tf_op jit(solution)/shard_map/ppermute | solution.py:305
  26.4 0.9 %all-to-all-done.refs_3_ = f32[32,4,1152]{2,1,0:T(4,128)S(1)} async-done(((f32[32,4,1152]{2,1,0:T(4,128)}), f32[32,4,1152]{2,1,0:T(4,128)S(1)}, u32[]{:S(2)}, u32[]{:S(2)}) %all-to-all-start) | async-done | bytes 589856 | tf_op jit(solution)/shard_map/all_to_all | solution.py:292
  27.3 2.2 %shard_map.156 = (bf16[32,40,128]{2,1,0:T(8,128)(2,1)}, f32[16,40,128]{2,1,0:T(8,128)}) custom-call(f32[16,40,128]{2,1,0:T(8,128)} %get-tuple-element.28.refs_0_, f32[16,40,128]{2,1,0:T(8,128)} %get-tuple-element.29.refs_1_, f32[4,48]{1,0:T(4,128)} %bitcast.16, f32[32,4,1152]{2,1,0:T(4,128)S(1)} %all-to-all-done.refs_3_), custom_call_target="tpu_custom_call" | custom-call | bytes 1901312 | tf_op jit(solution)/shard_map/pallas_call | solution.py:273
  29.5 1.1 %collective-permute-start.6 = (f32[16,40,128]{2,1,0:T(8,128)}, f32[16,40,128]{2,1,0:T(8,128)S(1)}, u32[]{:S(2)}, u32[]{:S(2)}) collective-permute-start(f32[16,40,128]{2,1,0:T(8,128)} %get-tuple-element.30.refs_0_), channel_id=1, source_target_pairs={{0,16},{16,0},{1,17},{17,1},{2,18},{18,2},{3,19},{19,3},{4,20},{20... | collective-permute-start | bytes 983048 | tf_op jit(solution)/shard_map/ppermute | solution.py:296
  30.6 0.0 collective-permute-done.3
  30.6 2.1 %collective-permute-start.4 = (f32[32,768]{1,0:T(8,128)S(1)}, f32[32,768]{1,0:T(8,128)S(1)}, u32[]{:S(2)}, u32[]{:S(2)}) collective-permute-start(f32[32,768]{1,0:T(8,128)S(1)} %add.18), channel_id=1, source_target_pairs={{0,8},{1,5},{2,10},{3,7},{4,12},{5,1},{6,14},{7,3},{8,0},{9,13},{1... | collective-permute-start | bytes 294920 | tf_op jit(solution)/shard_map/ppermute | solution.py:305
  32.7 3.2 %all-to-all-start.1 = ((bf16[32,40,128]{2,1,0:T(8,128)(2,1)}), bf16[32,40,128]{2,1,0:T(8,128)(2,1)S(1)}, u32[]{:S(2)}, u32[]{:S(2)}) async-start(bf16[32,40,128]{2,1,0:T(8,128)(2,1)} %get-tuple-element.40), calls=%async_computation.1 | async-start | bytes 655360 | tf_op jit(solution)/shard_map/all_to_all | solution.py:292
  36.0 1.3 %collective-permute-done.4 = f32[32,768]{1,0:T(8,128)S(1)} collective-permute-done((f32[32,768]{1,0:T(8,128)S(1)}, f32[32,768]{1,0:T(8,128)S(1)}, u32[]{:S(2)}, u32[]{:S(2)}) %collective-permute-start.4) | collective-permute-done | bytes 98336 | tf_op jit(solution)/shard_map/ppermute | solution.py:305
  37.3 0.1 collective-permute-start.5
  37.4 1.3 %collective-permute-done.5.other_ref = f32[32,768]{1,0:T(8,128)S(1)} collective-permute-done((f32[32,768]{1,0:T(8,128)S(1)}, f32[32,768]{1,0:T(8,128)S(1)}, u32[]{:S(2)}, u32[]{:S(2)}) %collective-permute-start.5) | collective-permute-done | bytes 98336 | tf_op jit(solution)/shard_map/ppermute | solution.py:300
  38.7 0.1 shard_map.157.refs_0_
  38.7 0.5 collective-permute-done.6.refs_1_
  39.2 2.7 %shard_map.159 = (f32[192,768]{1,0:T(8,128)}, f32[192,768]{1,0:T(8,128)}, f32[4,48]{1,0:T(4,128)}, f32[4,48]{1,0:T(4,128)}) custom-call(f32[16,40,128]{2,1,0:T(8,128)} %get-tuple-element.30.refs_0_, f32[16,40,128]{2,1,0:T(8,128)S(1)} %collective-permute-done.6.refs_1_, f32[192,768]{1,0:T(8,128)} %bitcast.10, f32[192,768]{1,0:T(8,128)} %bitcast.12, ...), custom_call_target="tpu_custom_call" | custom-call | bytes 3017728 | tf_op jit(solution)/shard_map/pallas_call | solution.py:273
  41.9 4.7 %shard_map.158 = (f32[960,768]{1,0:T(8,128)}, f32[960,768]{1,0:T(8,128)}) custom-call(bf16[192,768]{1,0:T(8,128)(2,1)S(1)} %shard_map.157.refs_0_, f32[64,960]{1,0:T(8,128)} %bitcast.15, f32[960,768]{1,0:T(8,128)} %refs_2_.1, f32[960,768]{1,0:T(8,128)} %refs_3_.1), custom_call_target="tpu_custom_call" | custom-call | flops 5096079360 | bytes 222068736 | tf_op jit(solution)/shard_map/pallas_call | solution.py:273
  46.6 1.1 %all-to-all-done.1.refs_0_ = bf16[32,40,128]{2,1,0:T(8,128)(2,1)S(1)} async-done(((bf16[32,40,128]{2,1,0:T(8,128)(2,1)}), bf16[32,40,128]{2,1,0:T(8,128)(2,1)S(1)}, u32[]{:S(2)}, u32[]{:S(2)}) %all-to-all-start.1) | async-done | bytes 327712 | tf_op jit(solution)/shard_map/all_to_all | solution.py:292
  47.7 0.9 %shard_map.160 = bf16[48,3072]{1,0:T(8,128)(2,1)} custom-call(bf16[32,40,128]{2,1,0:T(8,128)(2,1)S(1)} %all-to-all-done.1.refs_0_), custom_call_target="tpu_custom_call" | custom-call | bytes 622592 | tf_op jit(solution)/shard_map/pallas_call | solution.py:273
  (5 shorter events, 0.1 us)
Async XLA Ops:
  2.7 24.6 %all-to-all-start = ((f32[32,4,1152]{2,1,0:T(4,128)}), f32[32,4,1152]{2,1,0:T(4,128)S(1)}, u32[]{:S(2)}, u32[]{:S(2)}) async-start(f32[32,4,1152]{2,1,0:T(4,128)} %shard_map.155), calls=%async_computation | async-start | bytes 1179648 | tf_op jit(solution)/shard_map/all_to_all | solution.py:292
  13.1 1.4 %collective-permute-start = (f32[32,768]{1,0:T(8,128)S(1)}, f32[32,768]{1,0:T(8,128)S(1)}, u32[]{:S(2)}, u32[]{:S(2)}) collective-permute-start(f32[32,768]{1,0:T(8,128)S(1)} %get-tuple-element.25), channel_id=1, source_target_pairs={{0,1},{1,0},{2,3},{3,2},{4,5},{5,4},{6,7},{7,6},{8,9},{9,8},{10,11... | collective-permute-start | bytes 294920 | tf_op jit(solution)/shard_map/ppermute | solution.py:300
  14.5 5.4 %collective-permute-start.1 = (f32[32,768]{1,0:T(8,128)S(1)}, f32[32,768]{1,0:T(8,128)S(1)}, u32[]{:S(2)}, u32[]{:S(2)}) collective-permute-start(f32[32,768]{1,0:T(8,128)S(1)} %add.15), channel_id=1, source_target_pairs={{0,16},{1,3},{2,18},{3,1},{4,20},{5,7},{6,22},{7,5},{8,24},{9,11},... | collective-permute-start | bytes 294920 | tf_op jit(solution)/shard_map/ppermute | solution.py:305
  19.9 4.8 %collective-permute-start.2 = (f32[32,768]{1,0:T(8,128)S(1)}, f32[32,768]{1,0:T(8,128)S(1)}, u32[]{:S(2)}, u32[]{:S(2)}) collective-permute-start(f32[32,768]{1,0:T(8,128)S(1)} %add.16), channel_id=1, source_target_pairs={{0,2},{1,17},{2,0},{3,19},{4,6},{5,21},{6,4},{7,23},{8,10},{9,25},... | collective-permute-start | bytes 294920 | tf_op jit(solution)/shard_map/ppermute | solution.py:305
  24.6 6.0 %collective-permute-start.3 = (f32[32,768]{1,0:T(8,128)S(1)}, f32[32,768]{1,0:T(8,128)S(1)}, u32[]{:S(2)}, u32[]{:S(2)}) collective-permute-start(f32[32,768]{1,0:T(8,128)S(1)} %add.17), channel_id=1, source_target_pairs={{0,4},{1,9},{2,6},{3,11},{4,0},{5,13},{6,2},{7,15},{8,12},{9,1},{1... | collective-permute-start | bytes 294920 | tf_op jit(solution)/shard_map/ppermute | solution.py:305
  29.5 9.7 %collective-permute-start.6 = (f32[16,40,128]{2,1,0:T(8,128)}, f32[16,40,128]{2,1,0:T(8,128)S(1)}, u32[]{:S(2)}, u32[]{:S(2)}) collective-permute-start(f32[16,40,128]{2,1,0:T(8,128)} %get-tuple-element.30.refs_0_), channel_id=1, source_target_pairs={{0,16},{16,0},{1,17},{17,1},{2,18},{18,2},{3,19},{19,3},{4,20},{20... | collective-permute-start | bytes 983048 | tf_op jit(solution)/shard_map/ppermute | solution.py:296
  30.6 6.6 %collective-permute-start.4 = (f32[32,768]{1,0:T(8,128)S(1)}, f32[32,768]{1,0:T(8,128)S(1)}, u32[]{:S(2)}, u32[]{:S(2)}) collective-permute-start(f32[32,768]{1,0:T(8,128)S(1)} %add.18), channel_id=1, source_target_pairs={{0,8},{1,5},{2,10},{3,7},{4,12},{5,1},{6,14},{7,3},{8,0},{9,13},{1... | collective-permute-start | bytes 294920 | tf_op jit(solution)/shard_map/ppermute | solution.py:305
  32.7 14.9 %all-to-all-start.1 = ((bf16[32,40,128]{2,1,0:T(8,128)(2,1)}), bf16[32,40,128]{2,1,0:T(8,128)(2,1)S(1)}, u32[]{:S(2)}, u32[]{:S(2)}) async-start(bf16[32,40,128]{2,1,0:T(8,128)(2,1)} %get-tuple-element.40), calls=%async_computation.1 | async-start | bytes 655360 | tf_op jit(solution)/shard_map/all_to_all | solution.py:292
  37.3 1.4 %collective-permute-start.5 = (f32[32,768]{1,0:T(8,128)S(1)}, f32[32,768]{1,0:T(8,128)S(1)}, u32[]{:S(2)}, u32[]{:S(2)}) collective-permute-start(f32[32,768]{1,0:T(8,128)S(1)} %add.19.mine_ref), channel_id=1, source_target_pairs={{0,1},{1,0},{2,3},{3,2},{4,5},{5,4},{6,7},{7,6},{8,9},{9,8},{10,11... | collective-permute-start | bytes 294920 | tf_op jit(solution)/shard_map/ppermute | solution.py:300

commit v5 on v4

--- a/solution.py
+++ b/solution.py
@@ -165,8 +165,9 @@
         new = nesterov(outer, moment_ref[s], delta)[0].astype(bf16)
         send_ref[s] = new
         send_ref[shards + s] = new
-    store(0)
-    store(1)
+        if s % 4 == 3:
+            for n, at in ((0, s - 3), (0, shards + s - 3), (1, s - 3)):
+                store(n, slice(at, at + 4))
 
 
 def join_kernel(scale, mine_ref, other_ref, out_ref):
@@ -226,8 +227,8 @@
         cols = slice(LANES * k, LANES * k + LANES)
         for rows, part in ((slice(0, LANES), scr[cols, 0:LANES].T), (slice(LANES, LANES + HALF), scr[cols, LANES : 2 * LANES].T[:HALF])):
             new_ref[rows, cols], new_moment_ref[rows, cols] = nesterov(outer_ref[rows, cols], moment_ref[rows, cols], part)
-    store(0)
-    store(1)
+        store(0, (slice(None), cols))
+        store(1, (slice(None), cols))
     norms, width = outer_norm_ref.shape
     outer = outer_norm_ref[...]
     mine, other = (roll_half(ref[0, 32:40, :])[:norms, :width] for ref in (mine_ref, other_ref))

time: 48.9 us -> 48.9 us (level)
  transfers between devices with their start and end apart: 9 -> 9, of which waited for: 8 -> 8; matrix products, arithmetic and copies ran while one was open for 0% -> 0% of each run, Pallas kernels for 32% -> 31%
where the time goes in v5:
time: 48.9 us; the launch traced here: 48.6 us
  starting transfers between devices  19.6 us (40%)
  Pallas kernels  18.1 us (37%)
  waiting for transfers between devices  10.2 us (21%)
  between operations  0.74 us (2%)
    pallas_call x6, Pallas kernels, call(): pl.pallas_call(functools.partial(staged, kernel, parts, len(args) + len(o...  14.9 us
    all_to_all x2, starting transfers between devices, everyone(): lax.all_to_all(x, ('group', 'shard'), split_axis=0, concat_axis=0, tiled=...  10.7 us
    ppermute x4, starting transfers between devices, hop(): lax.ppermute(x, ('group', 'shard'), [(d, d ^ masks[d % 2]) for d in range...  7.4 us
    ppermute x4, waiting for transfers between devices, hop(): lax.ppermute(x, ('group', 'shard'), [(d, d ^ masks[d % 2]) for d in range...  5.12 us
    pallas_call x1, Pallas kernels, fast(): pl.pallas_call(coeff_kernel, out_shape=[jax.ShapeDtypeStruct((rank // 2,...  3.1 us
    all_to_all x2, waiting for transfers between devices, everyone(): lax.all_to_all(x, ('group', 'shard'), split_axis=0, concat_axis=0, tiled=...  2.36 us
    ppermute x2, waiting for transfers between devices, swap_shards(): lax.ppermute(x, 'shard', [(i, i ^ bit) for i in range(lax.axis_size('shar...  2.34 us
    ppermute x1, starting transfers between devices, swap_groups(): return lax.ppermute(x, 'group', [(0, 1), (1, 0)])  1.08 us
  transfers between devices with their start and end apart: 9, of which 8 were waited for; matrix products, arithmetic and copies ran while one was open for 0% of the time, Pallas kernels for 31%

profile of v5, /device:TPU:0, one launch (start us, length us, event | category | flops | bytes accessed | tf_op | source)
XLA Modules:
  0.0 48.6 jit_solution(6586026369288079249)
XLA Ops:
  0.6 2.0 %shard_map.155 = f32[32,4,1152]{2,1,0:T(4,128)} custom-call(f32[48,3072]{1,0:T(8,128)} %bitcast.13), custom_call_target="tpu_custom_call" | custom-call | bytes 1179648 | tf_op jit(solution)/shard_map/pallas_call | solution.py:274
  2.7 7.3 %all-to-all-start = ((f32[32,4,1152]{2,1,0:T(4,128)}), f32[32,4,1152]{2,1,0:T(4,128)S(1)}, u32[]{:S(2)}, u32[]{:S(2)}) async-start(f32[32,4,1152]{2,1,0:T(4,128)} %shard_map.155), calls=%async_computation | async-start | bytes 1179648 | tf_op jit(solution)/shard_map/all_to_all | solution.py:293
  10.0 3.1 %shard_map.153 = (f32[32,768]{1,0:T(8,128)S(1)}, f32[32,768]{1,0:T(8,128)S(1)}) custom-call(f32[64,960]{1,0:T(8,128)} %bitcast.14, f32[960,768]{1,0:T(8,128)} %refs_2_.1, f32[960,768]{1,0:T(8,128)} %bitcast.8), custom_call_target="tpu_custom_call" | custom-call | flops 283115520 | bytes 5898240 | tf_op jit(solution)/shard_map/pallas_call | solution.py:336
  13.1 0.3 collective-permute-start
  13.4 1.1 %collective-permute-done = f32[32,768]{1,0:T(8,128)S(1)} collective-permute-done((f32[32,768]{1,0:T(8,128)S(1)}, f32[32,768]{1,0:T(8,128)S(1)}, u32[]{:S(2)}, u32[]{:S(2)}) %collective-permute-start) | collective-permute-done | bytes 98336 | tf_op jit(solution)/shard_map/ppermute | solution.py:301
  14.5 1.8 %collective-permute-start.1 = (f32[32,768]{1,0:T(8,128)S(1)}, f32[32,768]{1,0:T(8,128)S(1)}, u32[]{:S(2)}, u32[]{:S(2)}) collective-permute-start(f32[32,768]{1,0:T(8,128)S(1)} %add.15), channel_id=1, source_target_pairs={{0,16},{1,3},{2,18},{3,1},{4,20},{5,7},{6,22},{7,5},{8,24},{9,11},... | collective-permute-start | bytes 294920 | tf_op jit(solution)/shard_map/ppermute | solution.py:306
  16.3 2.6 %shard_map.154 = (f32[16,40,128]{2,1,0:T(8,128)}, f32[16,40,128]{2,1,0:T(8,128)}) custom-call(f32[192,768]{1,0:T(8,128)} %bitcast.9, f32[192,768]{1,0:T(8,128)} %bitcast.11), custom_call_target="tpu_custom_call" | custom-call | bytes 1835008 | tf_op jit(solution)/shard_map/pallas_call | solution.py:274
  19.0 0.9 %collective-permute-done.1 = f32[32,768]{1,0:T(8,128)S(1)} collective-permute-done((f32[32,768]{1,0:T(8,128)S(1)}, f32[32,768]{1,0:T(8,128)S(1)}, u32[]{:S(2)}, u32[]{:S(2)}) %collective-permute-start.1) | collective-permute-done | bytes 98336 | tf_op jit(solution)/shard_map/ppermute | solution.py:306
  19.9 1.6 %collective-permute-start.2 = (f32[32,768]{1,0:T(8,128)S(1)}, f32[32,768]{1,0:T(8,128)S(1)}, u32[]{:S(2)}, u32[]{:S(2)}) collective-permute-start(f32[32,768]{1,0:T(8,128)S(1)} %add.16), channel_id=1, source_target_pairs={{0,2},{1,17},{2,0},{3,19},{4,6},{5,21},{6,4},{7,23},{8,10},{9,25},... | collective-permute-start | bytes 294920 | tf_op jit(solution)/shard_map/ppermute | solution.py:306
  21.5 3.1 %collective-permute-done.2 = f32[32,768]{1,0:T(8,128)S(1)} collective-permute-done((f32[32,768]{1,0:T(8,128)S(1)}, f32[32,768]{1,0:T(8,128)S(1)}, u32[]{:S(2)}, u32[]{:S(2)}) %collective-permute-start.2) | collective-permute-done | bytes 98336 | tf_op jit(solution)/shard_map/ppermute | solution.py:306
  24.6 1.8 %collective-permute-start.3 = (f32[32,768]{1,0:T(8,128)S(1)}, f32[32,768]{1,0:T(8,128)S(1)}, u32[]{:S(2)}, u32[]{:S(2)}) collective-permute-start(f32[32,768]{1,0:T(8,128)S(1)} %add.17), channel_id=1, source_target_pairs={{0,4},{1,9},{2,6},{3,11},{4,0},{5,13},{6,2},{7,15},{8,12},{9,1},{1... | collective-permute-start | bytes 294920 | tf_op jit(solution)/shard_map/ppermute | solution.py:306
  26.4 0.9 %all-to-all-done.refs_3_ = f32[32,4,1152]{2,1,0:T(4,128)S(1)} async-done(((f32[32,4,1152]{2,1,0:T(4,128)}), f32[32,4,1152]{2,1,0:T(4,128)S(1)}, u32[]{:S(2)}, u32[]{:S(2)}) %all-to-all-start) | async-done | bytes 589856 | tf_op jit(solution)/shard_map/all_to_all | solution.py:293
  27.3 2.1 %shard_map.156 = (bf16[32,40,128]{2,1,0:T(8,128)(2,1)}, f32[16,40,128]{2,1,0:T(8,128)}) custom-call(f32[16,40,128]{2,1,0:T(8,128)} %get-tuple-element.28.refs_0_, f32[16,40,128]{2,1,0:T(8,128)} %get-tuple-element.29.refs_1_, f32[4,48]{1,0:T(4,128)} %bitcast.16, f32[32,4,1152]{2,1,0:T(4,128)S(1)} %all-to-all-done.refs_3_), custom_call_target="tpu_custom_call" | custom-call | bytes 1901312 | tf_op jit(solution)/shard_map/pallas_call | solution.py:274
  29.4 1.1 %collective-permute-start.6 = (f32[16,40,128]{2,1,0:T(8,128)}, f32[16,40,128]{2,1,0:T(8,128)S(1)}, u32[]{:S(2)}, u32[]{:S(2)}) collective-permute-start(f32[16,40,128]{2,1,0:T(8,128)} %get-tuple-element.30.refs_0_), channel_id=1, source_target_pairs={{0,16},{16,0},{1,17},{17,1},{2,18},{18,2},{3,19},{19,3},{4,20},{20... | collective-permute-start | bytes 983048 | tf_op jit(solution)/shard_map/ppermute | solution.py:297
  30.5 0.0 collective-permute-done.3
  30.5 2.1 %collective-permute-start.4 = (f32[32,768]{1,0:T(8,128)S(1)}, f32[32,768]{1,0:T(8,128)S(1)}, u32[]{:S(2)}, u32[]{:S(2)}) collective-permute-start(f32[32,768]{1,0:T(8,128)S(1)} %add.18), channel_id=1, source_target_pairs={{0,8},{1,5},{2,10},{3,7},{4,12},{5,1},{6,14},{7,3},{8,0},{9,13},{1... | collective-permute-start | bytes 294920 | tf_op jit(solution)/shard_map/ppermute | solution.py:306
  32.6 3.4 %all-to-all-start.1 = ((bf16[32,40,128]{2,1,0:T(8,128)(2,1)}), bf16[32,40,128]{2,1,0:T(8,128)(2,1)S(1)}, u32[]{:S(2)}, u32[]{:S(2)}) async-start(bf16[32,40,128]{2,1,0:T(8,128)(2,1)} %get-tuple-element.40), calls=%async_computation.1 | async-start | bytes 655360 | tf_op jit(solution)/shard_map/all_to_all | solution.py:293
  36.0 1.1 %collective-permute-done.4 = f32[32,768]{1,0:T(8,128)S(1)} collective-permute-done((f32[32,768]{1,0:T(8,128)S(1)}, f32[32,768]{1,0:T(8,128)S(1)}, u32[]{:S(2)}, u32[]{:S(2)}) %collective-permute-start.4) | collective-permute-done | bytes 98336 | tf_op jit(solution)/shard_map/ppermute | solution.py:306
  37.2 0.1 collective-permute-start.5
  37.2 1.3 %collective-permute-done.5.other_ref = f32[32,768]{1,0:T(8,128)S(1)} collective-permute-done((f32[32,768]{1,0:T(8,128)S(1)}, f32[32,768]{1,0:T(8,128)S(1)}, u32[]{:S(2)}, u32[]{:S(2)}) %collective-permute-start.5) | collective-permute-done | bytes 98336 | tf_op jit(solution)/shard_map/ppermute | solution.py:301
  38.5 0.1 shard_map.157.refs_0_
  38.6 0.4 collective-permute-done.6.refs_1_
  38.9 2.5 %shard_map.159 = (f32[192,768]{1,0:T(8,128)}, f32[192,768]{1,0:T(8,128)}, f32[4,48]{1,0:T(4,128)}, f32[4,48]{1,0:T(4,128)}) custom-call(f32[16,40,128]{2,1,0:T(8,128)} %get-tuple-element.30.refs_0_, f32[16,40,128]{2,1,0:T(8,128)S(1)} %collective-permute-done.6.refs_1_, f32[192,768]{1,0:T(8,128)} %bitcast.10, f32[192,768]{1,0:T(8,128)} %bitcast.12, ...), custom_call_target="tpu_custom_call" | custom-call | bytes 3017728 | tf_op jit(solution)/shard_map/pallas_call | solution.py:274
  41.5 4.7 %shard_map.158 = (f32[960,768]{1,0:T(8,128)}, f32[960,768]{1,0:T(8,128)}) custom-call(bf16[192,768]{1,0:T(8,128)(2,1)S(1)} %shard_map.157.refs_0_, f32[64,960]{1,0:T(8,128)} %bitcast.15, f32[960,768]{1,0:T(8,128)} %refs_2_.1, f32[960,768]{1,0:T(8,128)} %refs_3_.1), custom_call_target="tpu_custom_call" | custom-call | flops 5096079360 | bytes 222068736 | tf_op jit(solution)/shard_map/pallas_call | solution.py:274
  46.2 1.5 %all-to-all-done.1.refs_0_ = bf16[32,40,128]{2,1,0:T(8,128)(2,1)S(1)} async-done(((bf16[32,40,128]{2,1,0:T(8,128)(2,1)}), bf16[32,40,128]{2,1,0:T(8,128)(2,1)S(1)}, u32[]{:S(2)}, u32[]{:S(2)}) %all-to-all-start.1) | async-done | bytes 327712 | tf_op jit(solution)/shard_map/all_to_all | solution.py:293
  47.7 0.9 %shard_map.160 = bf16[48,3072]{1,0:T(8,128)(2,1)} custom-call(bf16[32,40,128]{2,1,0:T(8,128)(2,1)S(1)} %all-to-all-done.1.refs_0_), custom_call_target="tpu_custom_call" | custom-call | bytes 622592 | tf_op jit(solution)/shard_map/pallas_call | solution.py:274
  (5 shorter events, 0.1 us)
Async XLA Ops:
  2.7 24.6 %all-to-all-start = ((f32[32,4,1152]{2,1,0:T(4,128)}), f32[32,4,1152]{2,1,0:T(4,128)S(1)}, u32[]{:S(2)}, u32[]{:S(2)}) async-start(f32[32,4,1152]{2,1,0:T(4,128)} %shard_map.155), calls=%async_computation | async-start | bytes 1179648 | tf_op jit(solution)/shard_map/all_to_all | solution.py:293
  13.1 1.4 %collective-permute-start = (f32[32,768]{1,0:T(8,128)S(1)}, f32[32,768]{1,0:T(8,128)S(1)}, u32[]{:S(2)}, u32[]{:S(2)}) collective-permute-start(f32[32,768]{1,0:T(8,128)S(1)} %get-tuple-element.25), channel_id=1, source_target_pairs={{0,1},{1,0},{2,3},{3,2},{4,5},{5,4},{6,7},{7,6},{8,9},{9,8},{10,11... | collective-permute-start | bytes 294920 | tf_op jit(solution)/shard_map/ppermute | solution.py:301
  14.5 5.4 %collective-permute-start.1 = (f32[32,768]{1,0:T(8,128)S(1)}, f32[32,768]{1,0:T(8,128)S(1)}, u32[]{:S(2)}, u32[]{:S(2)}) collective-permute-start(f32[32,768]{1,0:T(8,128)S(1)} %add.15), channel_id=1, source_target_pairs={{0,16},{1,3},{2,18},{3,1},{4,20},{5,7},{6,22},{7,5},{8,24},{9,11},... | collective-permute-start | bytes 294920 | tf_op jit(solution)/shard_map/ppermute | solution.py:306
  19.9 4.8 %collective-permute-start.2 = (f32[32,768]{1,0:T(8,128)S(1)}, f32[32,768]{1,0:T(8,128)S(1)}, u32[]{:S(2)}, u32[]{:S(2)}) collective-permute-start(f32[32,768]{1,0:T(8,128)S(1)} %add.16), channel_id=1, source_target_pairs={{0,2},{1,17},{2,0},{3,19},{4,6},{5,21},{6,4},{7,23},{8,10},{9,25},... | collective-permute-start | bytes 294920 | tf_op jit(solution)/shard_map/ppermute | solution.py:306
  24.6 5.9 %collective-permute-start.3 = (f32[32,768]{1,0:T(8,128)S(1)}, f32[32,768]{1,0:T(8,128)S(1)}, u32[]{:S(2)}, u32[]{:S(2)}) collective-permute-start(f32[32,768]{1,0:T(8,128)S(1)} %add.17), channel_id=1, source_target_pairs={{0,4},{1,9},{2,6},{3,11},{4,0},{5,13},{6,2},{7,15},{8,12},{9,1},{1... | collective-permute-start | bytes 294920 | tf_op jit(solution)/shard_map/ppermute | solution.py:306
  29.4 9.5 %collective-permute-start.6 = (f32[16,40,128]{2,1,0:T(8,128)}, f32[16,40,128]{2,1,0:T(8,128)S(1)}, u32[]{:S(2)}, u32[]{:S(2)}) collective-permute-start(f32[16,40,128]{2,1,0:T(8,128)} %get-tuple-element.30.refs_0_), channel_id=1, source_target_pairs={{0,16},{16,0},{1,17},{17,1},{2,18},{18,2},{3,19},{19,3},{4,20},{20... | collective-permute-start | bytes 983048 | tf_op jit(solution)/shard_map/ppermute | solution.py:297
  30.5 6.6 %collective-permute-start.4 = (f32[32,768]{1,0:T(8,128)S(1)}, f32[32,768]{1,0:T(8,128)S(1)}, u32[]{:S(2)}, u32[]{:S(2)}) collective-permute-start(f32[32,768]{1,0:T(8,128)S(1)} %add.18), channel_id=1, source_target_pairs={{0,8},{1,5},{2,10},{3,7},{4,12},{5,1},{6,14},{7,3},{8,0},{9,13},{1... | collective-permute-start | bytes 294920 | tf_op jit(solution)/shard_map/ppermute | solution.py:306
  32.6 15.1 %all-to-all-start.1 = ((bf16[32,40,128]{2,1,0:T(8,128)(2,1)}), bf16[32,40,128]{2,1,0:T(8,128)(2,1)S(1)}, u32[]{:S(2)}, u32[]{:S(2)}) async-start(bf16[32,40,128]{2,1,0:T(8,128)(2,1)} %get-tuple-element.40), calls=%async_computation.1 | async-start | bytes 655360 | tf_op jit(solution)/shard_map/all_to_all | solution.py:293
  37.2 1.4 %collective-permute-start.5 = (f32[32,768]{1,0:T(8,128)S(1)}, f32[32,768]{1,0:T(8,128)S(1)}, u32[]{:S(2)}, u32[]{:S(2)}) collective-permute-start(f32[32,768]{1,0:T(8,128)S(1)} %add.19.mine_ref), channel_id=1, source_target_pairs={{0,1},{1,0},{2,3},{3,2},{4,5},{5,4},{6,7},{7,6},{8,9},{9,8},{10,11... | collective-permute-start | bytes 294920 | tf_op jit(solution)/shard_map/ppermute | solution.py:301
